TPU v7x, 256 devices: a whole 4x4x8 slice. The times are simulated.
256 devices in a mesh: ctx: 64 (over y, z, core), kvg: 4 (over x).
Axes of the slice: x: 4, y: 4, z: 8, core: 2. Of those that a mesh axis runs over, the one named last changes fastest.
Arguments:
- tokens: bfloat16 [8192, 4096], P('ctx', 'kvg'), may hold values from -14 to 14
- questions: bfloat16 [512, 4096], P('ctx', 'kvg'), may hold values from -14 to 14
- q_weight: bfloat16 [4096, 2048], P(None, 'kvg'), may hold values from -0.09375 to 0.09375
- k_weight: bfloat16 [4096, 512], P(None, 'kvg'), may hold values from -0.09375 to 0.09375
- v_weight: bfloat16 [4096, 512], P(None, 'kvg'), may hold values from -0.09375 to 0.09375
- o_weight: bfloat16 [2048, 4096], P('kvg'), may hold values from -0.125 to 0.125
- anchor: int32 [1], replicated, may hold values from 0 to 63
- lengths: int32 [64], replicated, may hold values from 32 to 128, as said below
- positions: int32 [512], replicated, may hold values from 0 to 8191
Outputs:
- context_out: bfloat16 [8192, 4096], P('ctx', 'kvg')
- question_out: bfloat16 [512, 4096], P('ctx', 'kvg')
Inputs may be any that keep to these rules, and one draw needn't show every extreme that they name: `lengths`: every block has at least 32 valid tokens; some block is full and some block has exactly 32.
All inputs are finite; a program needn't handle non-finite values.
Results may differ from a plain program's by a relative error of at most 0.03.
Values may be sent and summed in bfloat16 or wider, within the bound.
A program may use at most 320 MiB of HBM per device.

v0:
```python
import math

import jax
import jax.numpy as jnp
from jax import lax
from jax.sharding import PartitionSpec as P

HEAD_DIM = 128


NEG_BIG = -1e30


def broadcast(block, axis, source):
    block = jnp.where(lax.axis_index(axis) == source, block, jnp.zeros_like(block))
    return lax.psum(block, axis)


def combined_all(array, axis, combine):
    everything = jax.tree.map(lambda part: lax.all_gather(part, axis), array)
    leading = jax.tree.map(lambda part: part[0], everything)

    def step(k, so_far):
        return combine(so_far, jax.tree.map(lambda part: part[k], everything))

    return lax.fori_loop(1, lax.axis_size(axis), step, leading)


def rotary(values, places):
    half_dim = values.shape[-1] // 2
    frequency = jnp.exp(
        jnp.arange(half_dim, dtype=jnp.float32) * (-2.0 * math.log(500000.0) / values.shape[-1])
    )
    angle = places.astype(jnp.float32)[:, None] * frequency[None, :]
    cosine = jnp.cos(angle)[:, None, :]
    sine = jnp.sin(angle)[:, None, :]
    front_part = values[..., :half_dim]
    back_part = values[..., half_dim:]
    return jnp.concatenate(
        [front_part * cosine - back_part * sine, back_part * cosine + front_part * sine], -1
    )


def combine_partials(earlier, later):
    max_one, total_one, weighted_one = earlier
    max_two, total_two, weighted_two = later
    joined = jnp.maximum(max_one, max_two)
    factor_one = jnp.exp(max_one - joined)
    factor_two = jnp.exp(max_two - joined)
    return (
        joined,
        total_one * factor_one + total_two * factor_two,
        weighted_one * factor_one[..., None] + weighted_two * factor_two[..., None],
    )


def local(tokens, questions, q_weight, k_weight, v_weight, o_weight, anchor, lengths, positions):
    row_count = tokens.shape[0]
    question_count = questions.shape[0]
    q_cols = q_weight.shape[1]
    kv_cols = k_weight.shape[1]
    kv_local = kv_cols // HEAD_DIM
    groups = q_cols // kv_cols
    scale = HEAD_DIM ** (-0.5)
    block_index = lax.axis_index("ctx")
    token_piece = lax.all_gather(tokens, "kvg", axis=1, tiled=True)
    question_piece = lax.all_gather(questions, "kvg", axis=1, tiled=True)
    token_q = jnp.dot(token_piece, q_weight, preferred_element_type=jnp.float32)
    token_k = jnp.dot(token_piece, k_weight, preferred_element_type=jnp.float32)
    token_v = jnp.dot(token_piece, v_weight, preferred_element_type=jnp.float32)
    question_q = jnp.dot(question_piece, q_weight, preferred_element_type=jnp.float32)
    token_places = block_index * row_count + jnp.arange(row_count, dtype=jnp.int32)
    query_rows = rotary(token_q.reshape(row_count, q_cols // HEAD_DIM, HEAD_DIM), token_places)
    query_rows = query_rows.astype(jnp.bfloat16).reshape(row_count, kv_local, groups, HEAD_DIM)
    key_local = rotary(token_k.reshape(row_count, kv_local, HEAD_DIM), token_places).astype(
        jnp.bfloat16
    )
    value_local = token_v.astype(jnp.bfloat16).reshape(row_count, kv_local, HEAD_DIM)
    question_places = lax.dynamic_slice_in_dim(
        positions, block_index * question_count, question_count, 0
    )
    question_rot = rotary(
        question_q.reshape(question_count, q_cols // HEAD_DIM, HEAD_DIM), question_places
    )
    question_rot = question_rot.astype(jnp.bfloat16).reshape(question_count, q_cols)
    anchor_index = anchor[0]
    anchor_keys, anchor_values = (
        broadcast(key_local, "ctx", anchor_index),
        broadcast(value_local, "ctx", anchor_index),
    )
    own_length = lax.dynamic_slice_in_dim(lengths, block_index, 1, 0)[0]
    anchor_length = lax.dynamic_slice_in_dim(lengths, anchor_index, 1, 0)[0]
    key_rows = jnp.concatenate([key_local, anchor_keys], 0)
    value_rows = jnp.concatenate([value_local, anchor_values], 0)
    query_pos = jnp.arange(row_count, dtype=jnp.int32)[:, None]
    key_pos = jnp.arange(2 * row_count, dtype=jnp.int32)[None, :]
    own_seen = (key_pos < row_count) & (key_pos <= query_pos) & (key_pos < own_length)
    far_seen = (
        (key_pos >= row_count)
        & (key_pos - row_count < anchor_length)
        & (block_index != anchor_index)
    )
    visible = own_seen | far_seen
    scores = (
        jnp.einsum("qkgd,skd->kgqs", query_rows, key_rows, preferred_element_type=jnp.float32)
        * scale
    )
    row_max = jnp.max(jnp.where(visible, scores, NEG_BIG), axis=-1, keepdims=True)
    weights = jnp.where(visible, jnp.exp(scores - row_max), 0.0)
    denominator = jnp.sum(weights, axis=-1)
    numerator = jnp.einsum(
        "kgqs,skd->qkgd",
        weights.astype(jnp.bfloat16),
        value_rows,
        preferred_element_type=jnp.float32,
    )
    attended = (
        (numerator / jnp.transpose(denominator, (2, 0, 1))[..., None])
        .astype(jnp.bfloat16)
        .reshape(row_count, q_cols)
    )
    whole_q = lax.all_gather(question_rot, "ctx", axis=0, tiled=True)
    whole_rows = whole_q.shape[0]
    whole_q = whole_q.reshape(whole_rows, kv_local, groups, HEAD_DIM)
    question_scores = (
        jnp.einsum("qkgd,skd->qkgs", whole_q, key_local, preferred_element_type=jnp.float32) * scale
    )
    local_index = jnp.arange(row_count, dtype=jnp.int32)
    question_seen = (
        (local_index < own_length)[None, :] & (token_places[None, :] <= positions[:, None])
    )[:, None, None, :]
    local_max = jnp.max(jnp.where(question_seen, question_scores, NEG_BIG), axis=-1)
    value_float = value_local.astype(jnp.float32)
    question_weights = jnp.where(
        question_seen, jnp.exp(question_scores - local_max[..., None]), 0.0
    )
    local_total = jnp.sum(question_weights, axis=-1)
    local_weighted = jnp.einsum(
        "qkgs,skd->qkgd", question_weights, value_float, precision=lax.Precision.HIGHEST
    )
    merged_max, merged_total, merged_weighted = combined_all(
        (local_max, local_total, local_weighted), "ctx", combine_partials
    )
    row_start = block_index * question_count
    own_total = lax.dynamic_slice_in_dim(merged_total, row_start, question_count, 0)
    own_weighted = lax.dynamic_slice_in_dim(merged_weighted, row_start, question_count, 0)
    question_att = (
        (own_weighted / own_total[..., None]).astype(jnp.bfloat16).reshape(question_count, q_cols)
    )
    token_term = jnp.dot(attended, o_weight, preferred_element_type=jnp.float32)
    question_term = jnp.dot(question_att, o_weight, preferred_element_type=jnp.float32)
    context_sum, question_sum = (
        lax.psum_scatter(
            token_term.astype(jnp.bfloat16), "kvg", scatter_dimension=1, tiled=True
        ).astype(jnp.float32),
        lax.psum_scatter(
            question_term.astype(jnp.bfloat16), "kvg", scatter_dimension=1, tiled=True
        ).astype(jnp.float32),
    )
    return (context_sum.astype(jnp.bfloat16), question_sum.astype(jnp.bfloat16))


def solution(mesh):
    in_specs = (
        P("ctx", "kvg"),
        P("ctx", "kvg"),
        P(None, "kvg"),
        P(None, "kvg"),
        P(None, "kvg"),
        P("kvg", None),
        P(),
        P(),
        P(),
    )
    out_specs = (P("ctx", "kvg"), P("ctx", "kvg"))
    return jax.shard_map(local, mesh=mesh, in_specs=in_specs, out_specs=out_specs, check_vma=False)
```

profile of v0, /device:TPU:1, one launch (start us, length us, event | category | flops | bytes accessed | tf_op | source)
XLA Modules:
  0.0 933.8 jit_solution(6705027661239783460)
XLA Ops:
  8.7 10.4 %all_gather.28 = bf16[8,4096]{1,0:T(8,128)(2,1)S(1)} all-gather(bf16[8,1024]{1,0:T(8,128)(2,1)} %param.12), channel_id=1, replica_groups=mesh['ctx'=64,'kvg'=4] {'kvg'}, dimensions={1}, use_global_device_ids=true | all-gather | bytes 81920 | tf_op jit(solution)/shard_map/all_gather | solution.py:67
  23.0 57.1 %all_gather.29 = bf16[512,512]{1,0:T(8,128)(2,1)S(1)} all-gather(bf16[8,512]{1,0:T(8,128)(2,1)S(1)} %maximum_bitcast_fusion.6), channel_id=1, replica_groups=mesh['ctx'=64,'kvg'=4] {'ctx'}, dimensions={0}, use_global_device_ids=true | all-gather | bytes 532480 | tf_op jit(solution)/shard_map/all_gather | solution.py:122
  96.9 53.7 %all-gather = f32[32768,4]{0,1:T(4,128)} all-gather(f32[512,4]{0,1:T(4,128)S(1)} %get-tuple-element.238), channel_id=2, replica_groups=mesh['ctx'=64,'kvg'=4] {'ctx'}, dimensions={0}, use_global_device_ids=true | all-gather | bytes 532480 | tf_op jit(solution)/shard_map/all_gather | solution.py:20
  150.8 48.2 %all-gather.1 = f32[32768,4]{0,1:T(4,128)S(1)} all-gather(f32[512,4]{0,1:T(4,128)S(1)} %fusion.10), channel_id=3, replica_groups=mesh['ctx'=64,'kvg'=4] {'ctx'}, dimensions={0}, use_global_device_ids=true | all-gather | bytes 532480 | tf_op jit(solution)/shard_map/all_gather | solution.py:20
  200.8 51.7 %all-reduce.3.cloned.1.call-done = (bf16[128,1,128]{0,2,1:T(8,128)(2,1)}, bf16[128,1,128]{2,0,1:T(8,128)(2,1)}) async-done(((bf16[128,1,128]{0,2,1:T(8,128)(2,1)}, bf16[128,1,128]{2,0,1:T(8,128)(2,1)}), (bf16[128,1,128]{0,2,1:T(8,128)(2,1)}, bf16[128,1,128]{2,0,1:T(8,128)(2,1)})) %all-reduce.3.cloned.1.call-update) | async-done | bytes 65552 | tf_op jit(solution)/shard_map/psum | solution.py:16
  254.7 3.9 convolution_convert_fusion
  258.7 230.1 %all-gather.8.cloned.1.call-done = f32[32768,1,4,128]{0,3,2,1:T(8,128)} async-done(((f32[512,1,4,128]{0,3,2,1:T(8,128)}), f32[32768,1,4,128]{0,3,2,1:T(8,128)}) %all-gather.8.cloned.1.call-update) | async-done | bytes 67108880 | tf_op jit(solution)/shard_map/all_gather | solution.py:20
  490.5 75.0 %copy.65 = f32[32768,1,4,128]{3,2,0,1:T(4,128)} copy(f32[32768,1,4,128]{0,3,2,1:T(8,128)} %all-gather.8.cloned.1.call-done) | data formatting | bytes 134217728 | tf_op jit(solution)/shard_map/while | solution.py:26
  565.5 340.7 %while.19 = (s32[]{:T(128)}, f32[512,1,4]{0,2,1:T(4,128)S(1)}, f32[512,1,4]{0,2,1:T(4,128)S(1)}, f32[512,1,4,128]{3,2,1,0:T(4,128)S(1)}, f32[64,512,1,4]{1,3,2,0...) while((s32[]{:T(128)}, f32[512,1,4]{0,2,1:T(4,128)S(1)}, ...), condition=%wide.region_8.9_spmd, body=%wide.region_7.8_spmd.sunk | while | flops 800773 | bytes 3301523 | solution.py:26
  567.3 3.6 fusion.74
  572.7 3.6 fusion.74
  578.1 3.6 fusion.74
  583.5 3.6 fusion.74
  588.9 3.6 fusion.74
  594.3 3.6 fusion.74
  599.7 3.6 fusion.74
  605.2 3.6 fusion.74
  610.6 3.6 fusion.74
  616.0 3.6 fusion.74
  621.4 3.6 fusion.74
  626.8 3.6 fusion.74
  632.2 3.6 fusion.74
  653.8 3.6 fusion.74
  659.2 3.6 fusion.74
  664.6 3.6 fusion.74
  670.1 3.6 fusion.74
  675.5 3.6 fusion.74
  680.9 3.6 fusion.74
  686.3 3.6 fusion.74
  691.7 3.6 fusion.74
  697.1 3.6 fusion.74
  910.0 17.3 %reduce-scatter.5.cloned.1.call-done = bf16[8,1024]{1,0:T(8,128)(2,1)} async-done(((bf16[8,4096]{1,0:T(8,128)(2,1)}), bf16[8,1024]{1,0:T(8,128)(2,1)}) %reduce-scatter.5.cloned.1.call-update) | async-done | bytes 16400 | tf_op jit(solution)/shard_map/reduce_scatter | solution.py:156
  (421 shorter events, 289.2 us)
Async XLA Ops:
  7.2 75.4 %copy-start = (bf16[4096,128]{1,0:T(8,128)(2,1)S(1)}, bf16[4096,128]{1,0:T(8,128)(2,1)}, u32[]{:S(2)}) copy-start(bf16[4096,128]{1,0:T(8,128)(2,1)} %param.15) | copy-start | bytes 3145732
  7.2 75.2 %copy-start.5 = (s32[512]{0:T(512)S(1)}, s32[512]{0:T(512)}, u32[]{:S(2)}) copy-start(s32[512]{0:T(512)} %param.19) | copy-start | bytes 6148
  7.2 73.9 %copy-start.6 = (s32[64]{0:T(128)S(1)}, s32[64]{0:T(128)}, u32[]{:S(2)}) copy-start(s32[64]{0:T(128)} %param.18) | copy-start | bytes 772
  7.2 75.3 %all-gather.6.cloned.1.call-start = ((), (), s32[]{:S(2)}) async-start(), calls=%async_computation.2 | async-start | bytes 1310720 | tf_op jit(solution)/shard_map/all_gather | solution.py:66
  7.9 76.9 %copy-start.2 = (bf16[4096,128]{1,0:T(8,128)(2,1)S(1)}, bf16[4096,128]{1,0:T(8,128)(2,1)}, u32[]{:S(2)}) copy-start(bf16[4096,128]{1,0:T(8,128)(2,1)} %param.14) | copy-start | bytes 3145732
  7.9 244.6 %all-reduce.3.cloned.1.call-start = ((), (), s32[]{:S(2)}) async-start(), calls=%async_computation.6 | async-start | bytes 131072 | tf_op jit(solution)/shard_map/psum | solution.py:16
  84.2 9.7 %copy-start.1 = (bf16[128,4096]{1,0:T(8,128)(2,1)S(1)}, bf16[128,4096]{1,0:T(8,128)(2,1)}, u32[]{:S(2)}) copy-start(bf16[128,4096]{1,0:T(8,128)(2,1)} %all-gather.6.cloned.1.call-done) | copy-start | bytes 3145732
  87.4 401.4 %all-gather.8.cloned.1.call-start = ((), (), s32[]{:S(2)}) async-start(), calls=%async_computation.5 | async-start | bytes 68157440 | tf_op jit(solution)/shard_map/all_gather | solution.py:20
  90.8 819.3 %reduce-scatter.3.cloned.1.call-start = ((), (), s32[]{:S(2)}) async-start(), calls=%async_computation.3 | async-start | bytes 1310720 | tf_op jit(solution)/shard_map/reduce_scatter | solution.py:153
  96.9 156.7 %copy-start.4 = (pred[128,256]{0,1:T(8,128)(4,1)S(1)}, pred[128,256]{0,1:T(8,128)(4,1)}, u32[]{:S(2)}) copy-start(pred[128,256]{0,1:T(8,128)(4,1)} %fusion.26) | copy-start | bytes 98308
  199.0 59.7 %copy-start.3 = (f32[32768,4]{0,1:T(4,128)}, f32[32768,4]{0,1:T(4,128)S(1)}, u32[]{:S(2)}) copy-start(f32[32768,4]{0,1:T(4,128)S(1)} %all-gather.1) | copy-start | bytes 1572868
  258.7 668.6 %reduce-scatter.5.cloned.1.call-start = ((), (), s32[]{:S(2)}) async-start(), calls=%async_computation.4 | async-start | bytes 81920 | tf_op jit(solution)/shard_map/reduce_scatter | solution.py:156
Sparse Core Ops, SparseCore 0:
  9.8 29.3 all-gather.5
  87.6 164.9 all-reduce.2
  255.3 233.4 all-gather.7
  491.8 21.2 reduce-scatter.2
  910.1 17.1 reduce-scatter.4
where the time goes:
time: 947 us; the launch traced here: 934 us
  other arithmetic  326 us (34%)
  waiting for transfers between devices  300 us (32%)
  blocking collectives  169 us (18%)
  local copies, waits for them, and re-layouts  98.2 us (10%)
  matrix products  21.9 us (2%)
  between operations  14.7 us (2%)
    all_gather x1, waiting for transfers between devices, combined_all(): everything = jax.tree.map(lambda part: lax.all_gather(part, axis), array)  230 us
    add x63, other arithmetic, combine_partials(): weighted_one * factor_one[..., None] + weighted_two * factor_two[..., None]  227 us
    all_gather x2, blocking collectives, combined_all(): everything = jax.tree.map(lambda part: lax.all_gather(part, axis), array)  102 us
    while x2, local copies, waits for them, and re-layouts, combined_all(): return lax.fori_loop(1, lax.axis_size(axis), step, leading)  75.4 us
    all_gather x1, blocking collectives, local(): whole_q = lax.all_gather(question_rot, 'ctx', axis=0, tiled=True)  57.1 us
    psum x1, waiting for transfers between devices, broadcast(): return lax.psum(block, axis)  51.7 us
    mul x63, other arithmetic, combine_partials(): weighted_two * factor_two[..., None]  46.8 us
    mul x63, other arithmetic, combine_partials(): weighted_one * factor_one[..., None] + weighted_two * factor_two[..., None]  44.8 us
  transfers between devices with their start and end apart: 5, of which 3 were waited for; matrix products, arithmetic and copies ran while one was open for 47% of the time, Pallas kernels for 0%

commit v1 on v0

v1 whole, which is shorter than its diff:
```python
import math

import jax
import jax.numpy as jnp
from jax import lax
from jax.experimental import pallas as pl
from jax.experimental.pallas import tpu as pltpu
from jax.sharding import PartitionSpec as P

HEAD_DIM = 128
NX = 4
NY, NZ, NC = 4, 8, 2
BLK = 128
QROW = 8
HEADS = 4
FEAT = 1024
QCOLS = HEADS * HEAD_DIM
WCOLS = QCOLS + 2 * HEAD_DIM
NEG_BIG = -1e30
SCALE = HEAD_DIM ** (-0.5)
F32 = jnp.float32
BF16 = jnp.bfloat16
MESH = pl.DeviceIdType.MESH
N_COPIES = 80
N_LOADS = 17


def dot_nn(a, b):
    return jnp.dot(a, b, preferred_element_type=F32)


def dot_nt(a, b):
    return lax.dot_general(a, b, (((1,), (1,)), ((), ())), preferred_element_type=F32)


def dot_tn(a, b):
    return lax.dot_general(a, b, (((0,), (0,)), ((), ())), preferred_element_type=F32)


def angles(places):
    lane = lax.broadcasted_iota(jnp.int32, places.shape, 1)
    half = HEAD_DIM // 2
    index = jnp.where(lane < half, lane, lane - half).astype(F32)
    frequency = jnp.exp(index * (-2.0 * math.log(500000.0) / HEAD_DIM))
    angle = places.astype(F32) * frequency
    sine = jnp.sin(angle)
    return jnp.cos(angle), jnp.where(lane < half, -sine, sine)


def rotate(head, cosine, sine):
    return head * cosine + pltpu.roll(head, HEAD_DIM // 2, 1) * sine


def kernel(
    tokens, questions, wq, wk, wv, wo, anchor, lengths, positions,
    ctx_out, q_out,
    w_in, w_out, tok, qpack, acc, q4, qz, kvb, a1, a2, anc,
    part, stats, part_in, stats_in, tr_out, tr_in, to_right, to_left, from_left, from_right,
    own_term, qx_out, qx_in, load_sem, send_sem, recv_sem,
):
    n_p = NY * NC
    piece = 2 * BLK // n_p
    c = lax.axis_index("ctx")
    g = lax.axis_index("kvg")
    core = lax.rem(c, NC)
    z = lax.rem(lax.div(c, NC), NZ)
    y = lax.div(c, NC * NZ)
    p = y * NC + core

    def at(y_, z_, core_):
        return (y_ * NZ + z_) * NC + core_

    src = [g, lax.rem(g + 3, NX), lax.rem(g + 1, NX), lax.rem(g + 2, NX)]
    left, right, opposite = (c, src[1]), (c, src[2]), (c, src[3])

    def p_peer(d):
        q = lax.rem(p + d, n_p)
        return (at(lax.div(q, NC), z, lax.rem(q, NC)), g)

    def z_peer(d):
        return (at(y, lax.rem(z + d, NZ), core), g)

    def y_peer(d):
        return (at(lax.rem(y + d, NY), z, core), g)

    sibling = (at(y, z, 1 - core), g)

    loads = []

    def load(source, target):
        copy = pltpu.make_async_copy(source, target, load_sem.at[len(loads)])
        copy.start()
        loads.append(copy)
        return copy

    tok_load = load(tokens, tok.at[0])
    w_loads = []
    for slot in range(NX):
        rows = pl.ds(pl.multiple_of(src[slot] * FEAT, FEAT), FEAT)
        w_loads.append([
            load(wq.at[rows, :], w_in.at[slot, :, pl.ds(0, QCOLS)]),
            load(wk.at[rows, :], w_in.at[slot, :, pl.ds(QCOLS, HEAD_DIM)]),
            load(wv.at[rows, :], w_in.at[slot, :, pl.ds(QCOLS + HEAD_DIM, HEAD_DIM)]),
        ])
    wo_loads = {}
    for slot in (3, 1, 2, 0):
        columns = pl.ds(pl.multiple_of(src[slot] * FEAT, FEAT), FEAT)
        wo_loads[slot] = load(wo.at[:, columns], w_out.at[slot])

    own_questions = questions[...].astype(F32)
    half_f = FEAT // 2
    qpack[0] = jnp.concatenate(
        [own_questions[:, :half_f], own_questions[:, half_f:]], axis=0
    ).astype(BF16)

    partners = [left, right, opposite]
    partners += [p_peer(d) for d in range(1, n_p)] + [z_peer(d) for d in range(1, NZ)]
    barrier = pltpu.get_barrier_semaphore()
    for partner in partners:
        pl.semaphore_signal(barrier, inc=1, device_id=partner, device_id_type=MESH)
    pl.semaphore_wait(barrier, len(partners))

    copies = []

    def send(source, target, device):
        index = len(copies)
        copy = pltpu.make_async_remote_copy(
            src_ref=source, dst_ref=target, send_sem=send_sem.at[index],
            recv_sem=recv_sem.at[index], device_id=device, device_id_type=MESH,
        )
        copy.start()
        copies.append(copy)
        return copy

    q_in = [
        send(qpack.at[0], qpack.at[1], right),
        send(qpack.at[0], qpack.at[2], left),
        send(qpack.at[0], qpack.at[3], opposite),
    ]
    top, bottom = pl.ds(0, BLK // 2), pl.ds(BLK // 2, BLK // 2)
    r_top = send(tokens.at[top], tok.at[1, top], right)
    l_bottom = send(tokens.at[bottom], tok.at[2, bottom], left)
    r_bottom = send(tokens.at[bottom], tok.at[1, bottom], right)
    l_top = send(tokens.at[top], tok.at[2, top], left)

    tok_load.wait()
    for copy in w_loads[0]:
        copy.wait()
    acc[...] = dot_nn(tok[0], w_in[0])
    row = lax.broadcasted_iota(jnp.int32, (BLK, HEAD_DIM), 0)
    cosine, sine = angles(row + c * BLK)
    q_row = lax.broadcasted_iota(jnp.int32, (QROW, HEAD_DIM), 0)
    q_places = jnp.zeros((QROW, HEAD_DIM), jnp.int32)
    for r in range(QROW):
        q_places = jnp.where(q_row == r, positions[c * QROW + r], q_places)
    q_cosine, q_sine = angles(q_places)

    for slot in range(1, NX):
        for copy in w_loads[slot]:
            copy.wait()
    q_total = jnp.zeros((2 * QROW, QCOLS), F32)
    for slot in (0, 1, 2, 3):
        if slot:
            q_in[slot - 1].wait_recv()
        packed = qpack[slot].astype(F32)
        rows = jnp.concatenate([packed[:QROW], packed[QROW:]], axis=1)
        rows = jnp.concatenate([rows, jnp.zeros_like(rows)], axis=0).astype(BF16)
        q_total = q_total + dot_nn(rows, w_in[slot, :, :QCOLS])
    q_heads = [
        rotate(q_total[:QROW, h * HEAD_DIM:(h + 1) * HEAD_DIM], q_cosine, q_sine)
        for h in range(HEADS)
    ]
    qz[0] = jnp.concatenate(q_heads, axis=0).astype(BF16)
    qz_in = [send(qz.at[0], qz.at[d], z_peer(d)) for d in range(1, NZ)]

    r_top.wait_recv()
    r_pass = send(tok.at[1, top], tok.at[3, top], right)
    l_bottom.wait_recv()
    l_pass = send(tok.at[2, bottom], tok.at[3, bottom], left)
    r_bottom.wait_recv()
    acc[...] += dot_nn(tok[1], w_in[1])
    l_top.wait_recv()
    acc[...] += dot_nn(tok[2], w_in[2])
    r_pass.wait_recv()
    l_pass.wait_recv()
    key_value = acc[:, QCOLS:] + dot_nn(tok[3], w_in[3, :, QCOLS:])
    kvb[0, 0, :BLK] = rotate(key_value[:, :HEAD_DIM], cosine, sine).astype(BF16)
    kvb[0, 0, BLK:] = key_value[:, HEAD_DIM:].astype(BF16)

    a1_in = []
    for d in range(1, n_p):
        there = pl.ds(pl.multiple_of(lax.rem(p + d, n_p) * piece, piece), piece)
        a1_in.append(send(kvb.at[0, 0, there], a1.at[d], p_peer(d)))
    kv_in = [send(kvb.at[0, 0], kvb.at[0, d], y_peer(d)) for d in range(1, NY)]

    for h in range(HEADS):
        columns = slice(h * HEAD_DIM, (h + 1) * HEAD_DIM)
        query = acc[:, columns] + dot_nn(tok[3], w_in[3, :, columns])
        q4[h * BLK:(h + 1) * BLK] = rotate(query, cosine, sine).astype(BF16)
    key_at = lax.broadcasted_iota(jnp.int32, (HEADS * BLK, BLK), 1)
    query_at = lax.rem(lax.broadcasted_iota(jnp.int32, (HEADS * BLK, BLK), 0), BLK)
    seen = (key_at <= query_at) & (key_at < lengths[c])
    scores = jnp.where(seen, dot_nt(q4[...], kvb[0, 0, :BLK]) * SCALE, NEG_BIG)
    own_max = jnp.max(scores, axis=1, keepdims=True)
    weights = jnp.where(seen, jnp.exp(scores - own_max), 0.0)
    own_sum = jnp.sum(weights, axis=1, keepdims=True)
    own_value = dot_nn(weights.astype(BF16), kvb[0, 0, BLK:])

    anchor_block = anchor[0]
    anchor_p = lax.div(anchor_block, NC * NZ) * NC + lax.rem(anchor_block, NC)
    anchor_z = lax.rem(lax.div(anchor_block, NC), NZ)

    def pick(chosen, wanted, index, block):
        here = jnp.zeros((piece, HEAD_DIM), jnp.int32) + wanted
        return jnp.where(here == index, block.astype(F32), chosen)

    mine = pl.ds(pl.multiple_of(p * piece, piece), piece)
    chosen = kvb[0, 0, mine].astype(F32)
    for d in range(1, n_p):
        a1_in[d - 1].wait_recv()
        chosen = pick(chosen, anchor_p, lax.rem(p + n_p - d, n_p), a1[d])
    a2[0] = chosen.astype(BF16)
    a2_in = [send(a2.at[0], a2.at[d], z_peer(d)) for d in range(1, NZ)]

    for copy in kv_in:
        copy.wait_recv()
    sib_in = send(kvb.at[0], kvb.at[1], sibling) if NC > 1 else None

    for d in range(1, NZ):
        a2_in[d - 1].wait_recv()
        chosen = pick(chosen, anchor_z, lax.rem(z + NZ - d, NZ), a2[d])
    anc[mine] = chosen.astype(BF16)
    a3_in = [send(anc.at[mine], anc.at[mine], p_peer(d)) for d in range(1, n_p)]

    n_q = NZ * HEADS * QROW
    lane = lax.broadcasted_iota(jnp.int32, (1, n_q), 1)
    reach = jnp.zeros((1, n_q), jnp.int32)
    for d in range(NZ):
        there = at(y, lax.rem(z + NZ - d, NZ), core) * QROW
        for r in range(QROW):
            spot = (lax.div(lane, HEADS * QROW) == d) & (lax.rem(lane, QROW) == r)
            reach = jnp.where(spot, positions[there + r], reach)
    for copy in qz_in:
        copy.wait_recv()
    queries = qz[...].reshape(n_q, HEAD_DIM)
    if sib_in is not None:
        sib_in.wait_recv()
    blocks = []
    key_row = lax.broadcasted_iota(jnp.int32, (BLK, n_q), 0)
    part_max = jnp.full((1, n_q), NEG_BIG, F32)
    for k in range(NC):
        for d in range(NY):
            number = at(lax.rem(y + NY - d, NY), z, core if k == 0 else 1 - core)
            visible = (key_row < lengths[number]) & (key_row + number * BLK <= reach)
            block_scores = dot_nt(kvb[k, d, :BLK], queries) * SCALE
            block_scores = jnp.where(visible, block_scores, NEG_BIG)
            part_max = jnp.maximum(part_max, jnp.max(block_scores, axis=0, keepdims=True))
            blocks.append((k, d, visible, block_scores))
    part_sum = jnp.zeros((1, n_q), F32)
    part_value = jnp.zeros((n_q, HEAD_DIM), F32)
    for k, d, visible, block_scores in blocks:
        block_weights = jnp.where(visible, jnp.exp(block_scores - part_max), 0.0)
        part_sum = part_sum + jnp.sum(block_weights, axis=0, keepdims=True)
        part_value = part_value + dot_tn(block_weights.astype(BF16), kvb[k, d, BLK:])
    n_r = HEADS * QROW
    part[...] = part_value.astype(BF16).reshape(NZ, n_r, HEAD_DIM)
    stats[0:1] = part_max
    stats[1:2] = part_sum
    stats[2:8] = jnp.zeros((6, n_q), F32)
    lanes = min(n_q, 128)
    part_ins = {}
    for d in range(1, NZ):
        back = z_peer(NZ - d)
        group = pl.ds(d * n_r // lanes * lanes, lanes)
        part_ins[NZ - d] = (
            send(part.at[d], part_in.at[NZ - d], back),
            send(stats.at[:, group], stats_in.at[NZ - d], back),
        )

    for copy in a3_in:
        copy.wait_recv()
    far = (key_at < lengths[anchor_block]) & (jnp.zeros_like(key_at) + anchor_block != c)
    scores = jnp.where(far, dot_nt(q4[...], anc[:BLK]) * SCALE, NEG_BIG)
    row_max = jnp.maximum(own_max, jnp.max(scores, axis=1, keepdims=True))
    weights = jnp.where(far, jnp.exp(scores - row_max), 0.0)
    own_factor = jnp.exp(own_max - row_max)
    total = jnp.sum(weights, axis=1, keepdims=True) + own_sum * own_factor
    value = dot_nn(weights.astype(BF16), anc[BLK:]) + own_value * own_factor
    value = (value / total).astype(BF16)
    attended = jnp.concatenate([value[h * BLK:(h + 1) * BLK] for h in range(HEADS)], axis=1)

    hb = BLK // 2
    wo_loads[3].wait()
    tr_out[...] = dot_nn(attended, w_out[3]).astype(BF16)
    tr_r = send(tr_out.at[top], tr_in.at[top], right)
    tr_l = send(tr_out.at[bottom], tr_in.at[bottom], left)
    wo_loads[2].wait()
    right_term = dot_nn(attended, w_out[2])
    to_right[hb:] = right_term[hb:].astype(BF16)
    pure_r = send(to_right.at[bottom], from_left.at[bottom], right)
    wo_loads[1].wait()
    left_term = dot_nn(attended, w_out[1])
    to_left[:hb] = left_term[:hb].astype(BF16)
    pure_l = send(to_left.at[top], from_right.at[top], left)
    wo_loads[0].wait()
    own_term[...] = dot_nn(attended, w_out[0])
    tr_r.wait_recv()
    to_right[:hb] = (right_term[:hb] + tr_in[:hb].astype(F32)).astype(BF16)
    sum_r = send(to_right.at[top], from_left.at[top], right)
    tr_l.wait_recv()
    to_left[hb:] = (left_term[hb:] + tr_in[hb:].astype(F32)).astype(BF16)
    sum_l = send(to_left.at[bottom], from_right.at[bottom], left)

    eye_row = lax.broadcasted_iota(jnp.int32, (n_r, lanes), 0)
    eye_lane = lax.broadcasted_iota(jnp.int32, (n_r, lanes), 1)

    def column(row_of_stats, slot):
        spot = eye_lane == eye_row + (slot * n_r) % lanes
        return jnp.sum(jnp.where(spot, row_of_stats, 0.0), axis=1, keepdims=True)

    maxima, sums, values = [], [], []
    for d in range(NZ):
        if d == 0:
            held, block = stats[:, 0:lanes], part[0]
        else:
            part_ins[d][0].wait_recv()
            part_ins[d][1].wait_recv()
            held, block = stats_in[d], part_in[d]
        slot = (NZ - d) % NZ
        maxima.append(column(held[0:1], slot))
        sums.append(column(held[1:2], slot))
        values.append(block.astype(F32))
    top_max = maxima[0]
    for one in maxima[1:]:
        top_max = jnp.maximum(top_max, one)
    all_sum = jnp.zeros((n_r, 1), F32)
    all_value = jnp.zeros((n_r, HEAD_DIM), F32)
    for one_max, one_sum, one_value in zip(maxima, sums, values):
        factor = jnp.exp(one_max - top_max)
        all_sum = all_sum + one_sum * factor
        all_value = all_value + one_value * factor
    all_value = all_value / all_sum
    q_att = jnp.concatenate([all_value[h * QROW:(h + 1) * QROW] for h in range(HEADS)], axis=1)
    q_att = jnp.concatenate([q_att, jnp.zeros_like(q_att)], axis=0).astype(BF16)
    qx_in_copies = []
    for slot, device in ((3, opposite), (2, right), (1, left)):
        term = dot_nn(q_att, w_out[slot])[:QROW]
        qx_out[slot] = jnp.concatenate([term[:, :half_f], term[:, half_f:]], axis=0).astype(BF16)
        qx_in_copies.append(send(qx_out.at[slot], qx_in.at[slot], device))
    q_own = dot_nn(q_att, w_out[0])[:QROW]

    for copy in (pure_r, pure_l, sum_r, sum_l):
        copy.wait_recv()
    ctx_out[...] = (
        own_term[...] + from_left[...].astype(F32) + from_right[...].astype(F32)
    ).astype(BF16)
    for copy in qx_in_copies:
        copy.wait_recv()
    for slot in (1, 2, 3):
        packed = qx_in[slot].astype(F32)
        q_own = q_own + jnp.concatenate([packed[:QROW], packed[QROW:]], axis=1)
    q_out[...] = q_own.astype(BF16)
    for copy in copies:
        copy.wait_send()


def local(tokens, questions, q_weight, k_weight, v_weight, o_weight, anchor, lengths, positions):
    n_q = NZ * HEADS * QROW
    n_r = HEADS * QROW
    lanes = min(n_q, 128)
    piece = 2 * BLK // (NY * NC)
    anywhere = pl.BlockSpec(memory_space=pl.ANY)
    vmem = pl.BlockSpec(memory_space=pltpu.VMEM)
    smem = pl.BlockSpec(memory_space=pltpu.SMEM)
    return pl.pallas_call(
        kernel,
        out_shape=(
            jax.ShapeDtypeStruct((BLK, FEAT), BF16),
            jax.ShapeDtypeStruct((QROW, FEAT), BF16),
        ),
        in_specs=[anywhere, vmem] + [anywhere] * 4 + [smem] * 3,
        out_specs=(vmem, vmem),
        scratch_shapes=[
            pltpu.VMEM((NX, FEAT, WCOLS), BF16),
            pltpu.VMEM((NX, QCOLS, FEAT), BF16),
            pltpu.VMEM((NX, BLK, FEAT), BF16),
            pltpu.VMEM((NX, 2 * QROW, FEAT // 2), BF16),
            pltpu.VMEM((BLK, WCOLS), F32),
            pltpu.VMEM((HEADS * BLK, HEAD_DIM), BF16),
            pltpu.VMEM((NZ, n_r, HEAD_DIM), BF16),
            pltpu.VMEM((NC, NY, 2 * BLK, HEAD_DIM), BF16),
            pltpu.VMEM((NY * NC, piece, HEAD_DIM), BF16),
            pltpu.VMEM((NZ, piece, HEAD_DIM), BF16),
            pltpu.VMEM((2 * BLK, HEAD_DIM), BF16),
            pltpu.VMEM((NZ, n_r, HEAD_DIM), BF16),
            pltpu.VMEM((8, n_q), F32),
            pltpu.VMEM((NZ, n_r, HEAD_DIM), BF16),
            pltpu.VMEM((NZ, 8, lanes), F32),
            pltpu.VMEM((BLK, FEAT), BF16),
            pltpu.VMEM((BLK, FEAT), BF16),
            pltpu.VMEM((BLK, FEAT), BF16),
            pltpu.VMEM((BLK, FEAT), BF16),
            pltpu.VMEM((BLK, FEAT), BF16),
            pltpu.VMEM((BLK, FEAT), BF16),
            pltpu.VMEM((BLK, FEAT), F32),
            pltpu.VMEM((NX, 2 * QROW, FEAT // 2), BF16),
            pltpu.VMEM((NX, 2 * QROW, FEAT // 2), BF16),
            pltpu.SemaphoreType.DMA((N_LOADS,)),
            pltpu.SemaphoreType.DMA((N_COPIES,)),
            pltpu.SemaphoreType.DMA((N_COPIES,)),
        ],
        compiler_params=pltpu.CompilerParams(
            collective_id=0, has_side_effects=True, vmem_limit_bytes=48 * 2**20
        ),
        name="fused_attention",
    )(tokens, questions, q_weight, k_weight, v_weight, o_weight, anchor, lengths, positions)


def solution(mesh):
    in_specs = (
        P("ctx", "kvg"),
        P("ctx", "kvg"),
        P(None, "kvg"),
        P(None, "kvg"),
        P(None, "kvg"),
        P("kvg", None),
        P(),
        P(),
        P(),
    )
    out_specs = (P("ctx", "kvg"), P("ctx", "kvg"))
    return jax.shard_map(local, mesh=mesh, in_specs=in_specs, out_specs=out_specs, check_vma=False)
```

time: 947 us -> 56.4 us (0.06); the launches traced: 934 us -> 56.1 us
  other arithmetic: 326 us -> 0 us
  waiting for transfers between devices: 300 us -> 0 us
  blocking collectives: 169 us -> 0 us
  local copies, waits for them, and re-layouts: 98.2 us -> 6.75 us
  Pallas kernels: 0 us -> 48 us
  matrix products: 21.9 us -> 0 us
  between operations: 14.7 us -> 1.3 us
    all_gather x2 -> x0, waiting for transfers between devices: 230 us -> none  [the longest x1 230 us: combined_all(): everything = jax.tree.map(lambda part: lax.all_gather(part, axis), array)]
    add x64 -> x0, other arithmetic: 227 us -> none  [the longest x63 227 us: combine_partials(): weighted_one * factor_one[..., None] + weighted_two * factor_two[..., None]]
    all_gather x4 -> x0, blocking collectives: 169 us -> none  [the longest x2 102 us: combined_all(): everything = jax.tree.map(lambda part: lax.all_gather(part, axis), array)]
    mul x126 -> x0, other arithmetic: 91.6 us -> none  [the longest x63 46.8 us: combine_partials(): weighted_two * factor_two[..., None]]
    while x65 -> x0, local copies, waits for them, and re-layouts: 75.5 us -> none  [the longest x2 75.4 us: combined_all(): return lax.fori_loop(1, lax.axis_size(axis), step, leading)]
    psum x1 -> x0, waiting for transfers between devices: 51.7 us -> none  [broadcast(): return lax.psum(block, axis)]
    pallas_call x0 -> x1, Pallas kernels: none -> 48 us  [local(): pl.pallas_call(kernel, out_shape=(jax.ShapeDtypeStruct((BLK, FEAT), BF16)...]
    dot_general x10 -> x0, matrix products: 21.9 us -> none  [the longest x1 3.92 us: local(): token_term = jnp.dot(attended, o_weight, preferred_element_type=jnp.float32)]
  transfers between devices with their start and end apart: 5 -> 0, of which waited for: 3 -> 0; matrix products, arithmetic and copies ran while one was open for 47% -> 0% of each run, Pallas kernels for 0% -> 0%
where the time goes in v1:
time: 56.4 us; the launch traced here: 56.1 us
  Pallas kernels  48 us (85%)
  local copies, waits for them, and re-layouts  6.75 us (12%)
  between operations  1.3 us (2%)
    pallas_call x1, Pallas kernels, local(): pl.pallas_call(kernel, out_shape=(jax.ShapeDtypeStruct((BLK, FEAT), BF16)...  48 us
    unnamed x14, local copies, waits for them, and re-layouts  6.75 us

profile of v1, /device:TPU:1, one launch (start us, length us, event | category | flops | bytes accessed | tf_op | source)
XLA Modules:
  0.0 56.1 jit_solution(5471573595536074970)
XLA Ops:
  1.3 0.0 copy-start
  1.3 1.2 %copy-done = bf16[4096,128]{1,0:T(8,128)(2,1)S(1)} copy-done((bf16[4096,128]{1,0:T(8,128)(2,1)S(1)}, bf16[4096,128]{1,0:T(8,128)(2,1)}, u32[]{:S(2)}) %copy-start) | copy-done | bytes 1048600
  2.5 0.0 copy-start.1
  2.5 1.2 %copy-done.1 = bf16[4096,128]{1,0:T(8,128)(2,1)S(1)} copy-done((bf16[4096,128]{1,0:T(8,128)(2,1)S(1)}, bf16[4096,128]{1,0:T(8,128)(2,1)}, u32[]{:S(2)}) %copy-start.1) | copy-done | bytes 1048600
  3.7 0.0 copy-start.2
  3.7 0.9 %copy-done.2 = bf16[128,1024]{1,0:T(8,128)(2,1)S(1)} copy-done((bf16[128,1024]{1,0:T(8,128)(2,1)S(1)}, bf16[128,1024]{1,0:T(8,128)(2,1)}, u32[]{:S(2)}) %copy-start.2) | copy-done | bytes 262168
  4.7 0.0 copy-start.3
  4.7 0.7 %copy-done.3 = bf16[8,1024]{1,0:T(8,128)(2,1)S(1)} copy-done((bf16[8,1024]{1,0:T(8,128)(2,1)S(1)}, bf16[8,1024]{1,0:T(8,128)(2,1)}, u32[]{:S(2)}) %copy-start.3) | copy-done | bytes 16408
  5.4 0.0 copy-start.4
  5.4 0.7 %copy-done.4 = s32[512]{0:T(512)S(1)} copy-done((s32[512]{0:T(512)S(1)}, s32[512]{0:T(512)}, u32[]{:S(2)}) %copy-start.4) | copy-done | bytes 2072
  6.1 0.0 copy-start.5
  6.1 0.7 %copy-done.5 = s32[64]{0:T(128)S(1)} copy-done((s32[64]{0:T(128)S(1)}, s32[64]{0:T(128)}, u32[]{:S(2)}) %copy-start.5) | copy-done | bytes 280
  6.7 48.0 %fused_attention.1 = (bf16[128,1024]{1,0:T(8,128)(2,1)S(1)}, bf16[8,1024]{1,0:T(8,128)(2,1)S(1)}) custom-call(bf16[128,1024]{1,0:T(8,128)(2,1)S(1)} %copy-done.2, bf16[8,1024]{1,0:T(8,128)(2,1)S(1)} %copy-done.3, bf16[4096,512]{1,0:T(8,128)(2,1)} %wq.1, bf16[4096,128]{1,0:T(8,128)(2,1)S(1)} %copy-done, bf16[4096,128]{1,0:T(8,128)(2,1)S(1)} %copy-done.1, ...), custom_call_target="tpu_custom_call" | custom-call | tf_op jit(solution)/shard_map/fused_attention/pallas_call | solution.py:375
  54.8 0.7 %copy.14 = bf16[128,1024]{1,0:T(8,128)(2,1)} copy(bf16[128,1024]{1,0:T(8,128)(2,1)S(1)} %get-tuple-element.4) | data formatting | bytes 524288
  55.5 0.6 %copy.15 = bf16[8,1024]{1,0:T(8,128)(2,1)} copy(bf16[8,1024]{1,0:T(8,128)(2,1)S(1)} %get-tuple-element.5) | data formatting | bytes 32768
Async XLA Ops:
  1.3 1.2 %copy-start = (bf16[4096,128]{1,0:T(8,128)(2,1)S(1)}, bf16[4096,128]{1,0:T(8,128)(2,1)}, u32[]{:S(2)}) copy-start(bf16[4096,128]{1,0:T(8,128)(2,1)} %wk.1) | copy-start | bytes 3145732
  2.5 1.2 %copy-start.1 = (bf16[4096,128]{1,0:T(8,128)(2,1)S(1)}, bf16[4096,128]{1,0:T(8,128)(2,1)}, u32[]{:S(2)}) copy-start(bf16[4096,128]{1,0:T(8,128)(2,1)} %wv.1) | copy-start | bytes 3145732
  3.7 0.9 %copy-start.2 = (bf16[128,1024]{1,0:T(8,128)(2,1)S(1)}, bf16[128,1024]{1,0:T(8,128)(2,1)}, u32[]{:S(2)}) copy-start(bf16[128,1024]{1,0:T(8,128)(2,1)} %tokens.1) | copy-start | bytes 786436
  4.7 0.7 %copy-start.3 = (bf16[8,1024]{1,0:T(8,128)(2,1)S(1)}, bf16[8,1024]{1,0:T(8,128)(2,1)}, u32[]{:S(2)}) copy-start(bf16[8,1024]{1,0:T(8,128)(2,1)} %questions.1) | copy-start | bytes 49156
  5.4 0.7 %copy-start.4 = (s32[512]{0:T(512)S(1)}, s32[512]{0:T(512)}, u32[]{:S(2)}) copy-start(s32[512]{0:T(512)} %positions.1) | copy-start | bytes 6148
  6.1 0.7 %copy-start.5 = (s32[64]{0:T(128)S(1)}, s32[64]{0:T(128)}, u32[]{:S(2)}) copy-start(s32[64]{0:T(128)} %lengths.1) | copy-start | bytes 772

commit v2 on v1

--- a/solution.py
+++ b/solution.py
@@ -22,7 +22,7 @@
 BF16 = jnp.bfloat16
 MESH = pl.DeviceIdType.MESH
 N_COPIES = 80
-N_LOADS = 17
+N_LOADS = 20
 
 
 def dot_nn(a, b):
@@ -54,7 +54,7 @@
 def kernel(
     tokens, questions, wq, wk, wv, wo, anchor, lengths, positions,
     ctx_out, q_out,
-    w_in, w_out, tok, qpack, acc, q4, qz, kvb, a1, a2, anc,
+    asked, lengths_s, positions_s, w_in, w_out, tok, qpack, acc, q4, qz, kvb, a1, a2, anc,
     part, stats, part_in, stats_in, tr_out, tr_in, to_right, to_left, from_left, from_right,
     own_term, qx_out, qx_in, load_sem, send_sem, recv_sem,
 ):
@@ -93,6 +93,8 @@
         loads.append(copy)
         return copy
 
+    asked_load = load(questions, asked)
+    scalar_loads = [load(lengths, lengths_s), load(positions, positions_s)]
     tok_load = load(tokens, tok.at[0])
     w_loads = []
     for slot in range(NX):
@@ -107,7 +109,8 @@
         columns = pl.ds(pl.multiple_of(src[slot] * FEAT, FEAT), FEAT)
         wo_loads[slot] = load(wo.at[:, columns], w_out.at[slot])
 
-    own_questions = questions[...].astype(F32)
+    asked_load.wait()
+    own_questions = asked[...].astype(F32)
     half_f = FEAT // 2
     qpack[0] = jnp.concatenate(
         [own_questions[:, :half_f], own_questions[:, half_f:]], axis=0
@@ -149,10 +152,12 @@
     acc[...] = dot_nn(tok[0], w_in[0])
     row = lax.broadcasted_iota(jnp.int32, (BLK, HEAD_DIM), 0)
     cosine, sine = angles(row + c * BLK)
+    for copy in scalar_loads:
+        copy.wait()
     q_row = lax.broadcasted_iota(jnp.int32, (QROW, HEAD_DIM), 0)
     q_places = jnp.zeros((QROW, HEAD_DIM), jnp.int32)
     for r in range(QROW):
-        q_places = jnp.where(q_row == r, positions[c * QROW + r], q_places)
+        q_places = jnp.where(q_row == r, positions_s[c * QROW + r], q_places)
     q_cosine, q_sine = angles(q_places)
 
     for slot in range(1, NX):
@@ -199,7 +204,7 @@
         q4[h * BLK:(h + 1) * BLK] = rotate(query, cosine, sine).astype(BF16)
     key_at = lax.broadcasted_iota(jnp.int32, (HEADS * BLK, BLK), 1)
     query_at = lax.rem(lax.broadcasted_iota(jnp.int32, (HEADS * BLK, BLK), 0), BLK)
-    seen = (key_at <= query_at) & (key_at < lengths[c])
+    seen = (key_at <= query_at) & (key_at < lengths_s[c])
     scores = jnp.where(seen, dot_nt(q4[...], kvb[0, 0, :BLK]) * SCALE, NEG_BIG)
     own_max = jnp.max(scores, axis=1, keepdims=True)
     weights = jnp.where(seen, jnp.exp(scores - own_max), 0.0)
@@ -239,7 +244,7 @@
         there = at(y, lax.rem(z + NZ - d, NZ), core) * QROW
         for r in range(QROW):
             spot = (lax.div(lane, HEADS * QROW) == d) & (lax.rem(lane, QROW) == r)
-            reach = jnp.where(spot, positions[there + r], reach)
+            reach = jnp.where(spot, positions_s[there + r], reach)
     for copy in qz_in:
         copy.wait_recv()
     queries = qz[...].reshape(n_q, HEAD_DIM)
@@ -251,7 +256,7 @@
     for k in range(NC):
         for d in range(NY):
             number = at(lax.rem(y + NY - d, NY), z, core if k == 0 else 1 - core)
-            visible = (key_row < lengths[number]) & (key_row + number * BLK <= reach)
+            visible = (key_row < lengths_s[number]) & (key_row + number * BLK <= reach)
             block_scores = dot_nt(kvb[k, d, :BLK], queries) * SCALE
             block_scores = jnp.where(visible, block_scores, NEG_BIG)
             part_max = jnp.maximum(part_max, jnp.max(block_scores, axis=0, keepdims=True))
@@ -279,7 +284,7 @@
 
     for copy in a3_in:
         copy.wait_recv()
-    far = (key_at < lengths[anchor_block]) & (jnp.zeros_like(key_at) + anchor_block != c)
+    far = (key_at < lengths_s[anchor_block]) & (jnp.zeros_like(key_at) + anchor_block != c)
     scores = jnp.where(far, dot_nt(q4[...], anc[:BLK]) * SCALE, NEG_BIG)
     row_max = jnp.maximum(own_max, jnp.max(scores, axis=1, keepdims=True))
     weights = jnp.where(far, jnp.exp(scores - row_max), 0.0)
@@ -369,18 +374,28 @@
     n_r = HEADS * QROW
     lanes = min(n_q, 128)
     piece = 2 * BLK // (NY * NC)
-    anywhere = pl.BlockSpec(memory_space=pl.ANY)
+    anywhere = pl.BlockSpec(memory_space=pltpu.HBM)
     vmem = pl.BlockSpec(memory_space=pltpu.VMEM)
     smem = pl.BlockSpec(memory_space=pltpu.SMEM)
+    operands = [
+        pltpu.with_memory_space_constraint(x, pltpu.HBM)
+        for x in (tokens, questions, q_weight, k_weight, v_weight, o_weight)
+    ]
+    lengths, positions = [
+        pltpu.with_memory_space_constraint(x, pltpu.HBM) for x in (lengths, positions)
+    ]
     return pl.pallas_call(
         kernel,
         out_shape=(
             jax.ShapeDtypeStruct((BLK, FEAT), BF16),
             jax.ShapeDtypeStruct((QROW, FEAT), BF16),
         ),
-        in_specs=[anywhere, vmem] + [anywhere] * 4 + [smem] * 3,
+        in_specs=[anywhere] * 6 + [smem] + [anywhere] * 2,
         out_specs=(vmem, vmem),
         scratch_shapes=[
+            pltpu.VMEM((QROW, FEAT), BF16),
+            pltpu.SMEM(lengths.shape, jnp.int32),
+            pltpu.SMEM(positions.shape, jnp.int32),
             pltpu.VMEM((NX, FEAT, WCOLS), BF16),
             pltpu.VMEM((NX, QCOLS, FEAT), BF16),
             pltpu.VMEM((NX, BLK, FEAT), BF16),
@@ -410,10 +425,10 @@
             pltpu.SemaphoreType.DMA((N_COPIES,)),
         ],
         compiler_params=pltpu.CompilerParams(
-            collective_id=0, has_side_effects=True, vmem_limit_bytes=48 * 2**20
+            collective_id=0, has_side_effects=True, vmem_limit_bytes=40 * 2**20
         ),
         name="fused_attention",
-    )(tokens, questions, q_weight, k_weight, v_weight, o_weight, anchor, lengths, positions)
+    )(*operands, anchor, lengths, positions)
 
 
 def solution(mesh):

time: 56.4 us -> 50.6 us (0.90)
  local copies, waits for them, and re-layouts: 6.75 us -> 1.31 us
    unnamed x14 -> x2, local copies, waits for them, and re-layouts: 6.75 us -> 1.31 us
where the time goes in v2:
time: 50.6 us; the launch traced here: 50.4 us
  Pallas kernels  47.8 us (94%)
  local copies, waits for them, and re-layouts  1.31 us (3%)
  between operations  1.29 us (3%)
    pallas_call x1, Pallas kernels, local(): pl.pallas_call(kernel, out_shape=(jax.ShapeDtypeStruct((BLK, FEAT), BF16)...  47.8 us
    unnamed x2, local copies, waits for them, and re-layouts  1.31 us

profile of v2, /device:TPU:1, one launch (start us, length us, event | category | flops | bytes accessed | tf_op | source)
XLA Modules:
  0.0 50.4 jit_solution(13678827952169304249)
XLA Ops:
  1.3 47.8 %fused_attention.1 = (bf16[128,1024]{1,0:T(8,128)(2,1)S(1)}, bf16[8,1024]{1,0:T(8,128)(2,1)S(1)}) custom-call(bf16[128,1024]{1,0:T(8,128)(2,1)} %tokens.1, bf16[8,1024]{1,0:T(8,128)(2,1)} %questions.1, bf16[4096,512]{1,0:T(8,128)(2,1)} %wq.1, bf16[4096,128]{1,0:T(8,128)(2,1)} %wk.1, bf16[4096,128]{1,0:T(8,128)(2,1)} %wv.1, bf16[512,4096]{1,0:T(8,128)(2,1)} %wo.1, ...), custom_call_target="tpu_custom_call" | custom-call | tf_op jit(solution)/shard_map/fused_attention/pallas_call | solution.py:387
  49.1 0.7 %copy.14 = bf16[128,1024]{1,0:T(8,128)(2,1)} copy(bf16[128,1024]{1,0:T(8,128)(2,1)S(1)} %get-tuple-element.4) | data formatting | bytes 524288
  49.8 0.6 %copy.15 = bf16[8,1024]{1,0:T(8,128)(2,1)} copy(bf16[8,1024]{1,0:T(8,128)(2,1)S(1)} %get-tuple-element.5) | data formatting | bytes 32768

commit v3 on v2

v3 whole, which is shorter than its diff:
```python
import math

import jax
import jax.numpy as jnp
from jax import lax
from jax.experimental import pallas as pl
from jax.experimental.pallas import tpu as pltpu
from jax.sharding import PartitionSpec as P

HEAD_DIM = 128
NX = 4
NY, NZ, NC = 4, 8, 2
BLK = 128
QROW = 8
HEADS = 4
FEAT = 1024
QCOLS = HEADS * HEAD_DIM
WCOLS = QCOLS + 2 * HEAD_DIM
NEG_BIG = -1e30
SCALE = HEAD_DIM ** (-0.5)
F32 = jnp.float32
BF16 = jnp.bfloat16
MESH = pl.DeviceIdType.MESH
LANES = 128
N_COPIES = 96
N_LOADS = 20


def dot_nn(a, b):
    return jnp.dot(a, b, preferred_element_type=F32)


def dot_nt(a, b):
    return lax.dot_general(a, b, (((1,), (1,)), ((), ())), preferred_element_type=F32)


def dot_tn(a, b):
    return lax.dot_general(a, b, (((0,), (0,)), ((), ())), preferred_element_type=F32)


def angles(places):
    lane = lax.broadcasted_iota(jnp.int32, places.shape, 1)
    half = HEAD_DIM // 2
    index = jnp.where(lane < half, lane, lane - half).astype(F32)
    frequency = jnp.exp(index * (-2.0 * math.log(500000.0) / HEAD_DIM))
    angle = places.astype(F32) * frequency
    sine = jnp.sin(angle)
    return jnp.cos(angle), jnp.where(lane < half, -sine, sine)


def rotate(head, cosine, sine):
    return head * cosine + pltpu.roll(head, HEAD_DIM // 2, 1) * sine


def kernel(
    tokens, questions, wq, wk, wv, wo, anchor, lengths, positions,
    ctx_out, q_out,
    asked, lengths_s, positions_s, w_in, w_out, own_tok, tok, qpack, acc, q4, qz, kvb,
    a_rows, a_tok, a2, anc, part, part_in, tr_out, tr_in, to_right, to_left,
    from_left, from_right, own_term, qx_out, qx_in, load_sem, send_sem, recv_sem,
):
    n_p = NY * NC
    a_len = BLK // n_p
    c = lax.axis_index("ctx")
    g = lax.axis_index("kvg")
    core = lax.rem(c, NC)
    z = lax.rem(lax.div(c, NC), NZ)
    y = lax.div(c, NC * NZ)
    p = y * NC + core

    def at(y_, z_, core_):
        return (y_ * NZ + z_) * NC + core_

    src = [g, lax.rem(g + 3, NX), lax.rem(g + 1, NX), lax.rem(g + 2, NX)]
    left, right, opposite = (c, src[1]), (c, src[2]), (c, src[3])

    def flip(dc):
        return 1 - core if dc else core

    p_steps = [(dy, dc) for dy in range(NY) for dc in range(NC) if dy or dc]
    p_steps.sort(key=lambda s: (-min(s[0], NY - s[0]), -s[1]))
    z_steps = sorted(range(1, NZ), key=lambda d: -min(d, NZ - d))

    def p_peer(dy, dc):
        return (at(lax.rem(y + dy, NY), z, flip(dc)), g)

    def p_index(dy, dc):
        return lax.rem(y + dy, NY) * NC + flip(dc)

    def z_peer(d):
        return (at(y, lax.rem(z + d, NZ), core), g)

    loads = []

    def load(source, target):
        copy = pltpu.make_async_copy(source, target, load_sem.at[len(loads)])
        copy.start()
        loads.append(copy)
        return copy

    asked_load = load(questions, asked)
    scalar_loads = [load(lengths, lengths_s), load(positions, positions_s)]
    tok_load = load(tokens, own_tok)
    w_loads = []
    for slot in range(NX):
        rows = pl.ds(pl.multiple_of(src[slot] * FEAT, FEAT), FEAT)
        w_loads.append([
            load(wq.at[rows, :], w_in.at[slot, :, pl.ds(0, QCOLS)]),
            load(wk.at[rows, :], w_in.at[slot, :, pl.ds(QCOLS, HEAD_DIM)]),
            load(wv.at[rows, :], w_in.at[slot, :, pl.ds(QCOLS + HEAD_DIM, HEAD_DIM)]),
        ])

    partners = [z_peer(d) for d in z_steps] + [opposite]
    partners += [p_peer(dy, dc) for dy, dc in p_steps] + [left, right]
    barrier = pltpu.get_barrier_semaphore()
    for partner in partners:
        pl.semaphore_signal(barrier, inc=1, device_id=partner, device_id_type=MESH)

    asked_load.wait()
    own_questions = asked[...].astype(F32)
    half_f = FEAT // 2
    qpack[0] = jnp.concatenate(
        [own_questions[:, :half_f], own_questions[:, half_f:]], axis=0
    ).astype(BF16)
    pl.semaphore_wait(barrier, len(partners))

    copies = []

    def send(source, target, device):
        index = len(copies)
        copy = pltpu.make_async_remote_copy(
            src_ref=source, dst_ref=target, send_sem=send_sem.at[index],
            recv_sem=recv_sem.at[index], device_id=device, device_id_type=MESH,
        )
        copy.start()
        copies.append(copy)
        return copy

    quarter = FEAT // 4
    near_r, near_l = {}, {}

    def send_tokens(j_r, j_l):
        near_r[j_r] = send(tokens.at[:, pl.ds(j_r * quarter, quarter)], tok.at[1, j_r], right)
        near_l[j_l] = send(tokens.at[:, pl.ds(j_l * quarter, quarter)], tok.at[2, j_l], left)

    send_tokens(0, 3)
    a_in = {}
    for dy, dc in p_steps:
        there = pl.ds(pl.multiple_of(p_index(dy, dc) * a_len, a_len), a_len)
        a_in[dy, dc] = send(tokens.at[there, :], a_rows.at[dy * NC + dc], p_peer(dy, dc))
    send_tokens(1, 2)
    send_tokens(2, 1)
    send_tokens(3, 0)
    q_in = [
        send(qpack.at[0], qpack.at[3], opposite),
        send(qpack.at[0], qpack.at[1], right),
        send(qpack.at[0], qpack.at[2], left),
    ]

    tok_load.wait()
    for copy in w_loads[0]:
        copy.wait()
    acc[...] = dot_nn(own_tok[...], w_in[0])
    row = lax.broadcasted_iota(jnp.int32, (BLK, HEAD_DIM), 0)
    cosine, sine = angles(row + c * BLK)
    for copy in scalar_loads:
        copy.wait()
    q_row = lax.broadcasted_iota(jnp.int32, (QROW, HEAD_DIM), 0)
    q_places = jnp.zeros((QROW, HEAD_DIM), jnp.int32)
    for r in range(QROW):
        q_places = jnp.where(q_row == r, positions_s[c * QROW + r], q_places)
    q_cosine, q_sine = angles(q_places)
    anchor_block = anchor[0]
    anchor_y = lax.div(anchor_block, NC * NZ)
    anchor_core = lax.rem(anchor_block, NC)
    anchor_z = lax.rem(lax.div(anchor_block, NC), NZ)
    a_row = lax.broadcasted_iota(jnp.int32, (a_len, HEAD_DIM), 0)
    a_cosine, a_sine = angles(a_row + p * a_len + anchor_block * BLK)

    far_r, far_l = {}, {}

    def pass_on(j_r, j_l):
        near_r[j_r].wait_recv()
        far_r[j_r] = send(tok.at[1, j_r], tok.at[3, j_r], right)
        near_l[j_l].wait_recv()
        far_l[j_l] = send(tok.at[2, j_l], tok.at[3, j_l], left)

    pass_on(0, 3)
    pass_on(1, 2)

    wanted = jnp.zeros((a_len, FEAT), jnp.int32)
    wanted_p = wanted + (anchor_y * NC + anchor_core)
    chosen = own_tok[pl.ds(pl.multiple_of(p * a_len, a_len), a_len), :].astype(F32)
    for dy, dc in p_steps:
        a_in[dy, dc].wait_recv()
        origin = lax.rem(y + NY - dy, NY) * NC + flip(dc)
        chosen = jnp.where(wanted_p == origin, a_rows[dy * NC + dc].astype(F32), chosen)
    a_tok[0] = chosen.astype(BF16)
    at_in = [
        send(a_tok.at[0], a_tok.at[3], opposite),
        send(a_tok.at[0], a_tok.at[1], right),
        send(a_tok.at[0], a_tok.at[2], left),
    ]

    for slot in (1, 2):
        for copy in w_loads[slot]:
            copy.wait()
    for j in range(2):
        acc[...] += dot_nn(tok[1, j], w_in[1, j * quarter:(j + 1) * quarter])
        k = 3 - j
        acc[...] += dot_nn(tok[2, k], w_in[2, k * quarter:(k + 1) * quarter])
    for j in range(2, 4):
        near_r[j].wait_recv()
        acc[...] += dot_nn(tok[1, j], w_in[1, j * quarter:(j + 1) * quarter])
        k = 3 - j
        near_l[k].wait_recv()
        acc[...] += dot_nn(tok[2, k], w_in[2, k * quarter:(k + 1) * quarter])

    for copy in w_loads[3]:
        copy.wait()
    for copy in q_in:
        copy.wait_recv()
    q_total = jnp.zeros((2 * QROW, QCOLS), F32)
    for slot in range(NX):
        packed = qpack[slot].astype(F32)
        rows = jnp.concatenate([packed[:QROW], packed[QROW:]], axis=1)
        rows = jnp.concatenate([rows, jnp.zeros_like(rows)], axis=0).astype(BF16)
        q_total = q_total + dot_nn(rows, w_in[slot, :, :QCOLS])
    q_heads = [
        rotate(q_total[:QROW, h * HEAD_DIM:(h + 1) * HEAD_DIM], q_cosine, q_sine)
        for h in range(HEADS)
    ]
    qz[0] = jnp.concatenate(q_heads, axis=0).astype(BF16)
    qz_in = [send(qz.at[0], qz.at[d], z_peer(d)) for d in z_steps]

    key_value = acc[:, QCOLS:]
    for j in (0, 3, 1, 2):
        (far_r if j < 2 else far_l)[j].wait_recv()
        key_value = key_value + dot_nn(tok[3, j], w_in[3, j * quarter:(j + 1) * quarter, QCOLS:])
    kvb[0, 0, :BLK] = rotate(key_value[:, :HEAD_DIM], cosine, sine).astype(BF16)
    kvb[0, 0, BLK:] = key_value[:, HEAD_DIM:].astype(BF16)

    for copy in at_in:
        copy.wait_recv()
    a_kv = jnp.zeros((a_len, 2 * HEAD_DIM), F32)
    for slot in range(NX):
        a_kv = a_kv + dot_nn(a_tok[slot], w_in[slot, :, QCOLS:])
    a2[0, :a_len] = rotate(a_kv[:, :HEAD_DIM], a_cosine, a_sine).astype(BF16)
    a2[0, a_len:] = a_kv[:, HEAD_DIM:].astype(BF16)
    a2_in = {d: send(a2.at[0], a2.at[d], z_peer(d)) for d in z_steps}
    kv_in = [
        send(kvb.at[0, 0], kvb.at[0, d], p_peer(d, 0))
        for d in sorted(range(1, NY), key=lambda d: -min(d, NY - d))
    ]
    wo_loads = {}
    for slot in (3, 2, 1, 0):
        columns = pl.ds(pl.multiple_of(src[slot] * FEAT, FEAT), FEAT)
        wo_loads[slot] = load(wo.at[:, columns], w_out.at[slot])

    for h in range(HEADS):
        columns = slice(h * HEAD_DIM, (h + 1) * HEAD_DIM)
        query = acc[:, columns]
        for j in range(4):
            query = query + dot_nn(tok[3, j], w_in[3, j * quarter:(j + 1) * quarter, columns])
        q4[h * BLK:(h + 1) * BLK] = rotate(query, cosine, sine).astype(BF16)
    key_at = lax.broadcasted_iota(jnp.int32, (HEADS * BLK, BLK), 1)
    query_at = lax.rem(lax.broadcasted_iota(jnp.int32, (HEADS * BLK, BLK), 0), BLK)
    seen = (key_at <= query_at) & (key_at < lengths_s[c])
    scores = jnp.where(seen, dot_nt(q4[...], kvb[0, 0, :BLK]) * SCALE, NEG_BIG)
    own_max = jnp.max(scores, axis=1, keepdims=True)
    weights = jnp.where(seen, jnp.exp(scores - own_max), 0.0)
    own_sum = jnp.sum(weights, axis=1, keepdims=True)
    own_value = dot_nn(weights.astype(BF16), kvb[0, 0, BLK:])

    n_q = NZ * HEADS * QROW
    lane = lax.broadcasted_iota(jnp.int32, (1, n_q), 1)
    reach = jnp.zeros((1, n_q), jnp.int32)
    for d in range(NZ):
        there = at(y, lax.rem(z + NZ - d, NZ), core) * QROW
        for r in range(QROW):
            spot = (lax.div(lane, HEADS * QROW) == d) & (lax.rem(lane, QROW) == r)
            reach = jnp.where(spot, positions_s[there + r], reach)

    for copy in kv_in:
        copy.wait_recv()
    sib_in = send(kvb.at[0], kvb.at[1], (at(y, z, 1 - core), g)) if NC > 1 else None
    wanted_z = jnp.zeros((2 * a_len, HEAD_DIM), jnp.int32) + anchor_z
    chosen = a2[0].astype(F32)
    for d in z_steps:
        a2_in[d].wait_recv()
        origin = lax.rem(z + NZ - d, NZ)
        chosen = jnp.where(wanted_z == origin, a2[d].astype(F32), chosen)
    anc[p] = chosen.astype(BF16)
    a3_in = [send(anc.at[p], anc.at[p], p_peer(dy, dc)) for dy, dc in p_steps]

    for copy in qz_in:
        copy.wait_recv()
    queries = qz[...].reshape(n_q, HEAD_DIM)
    if sib_in is not None:
        sib_in.wait_recv()
    blocks = []
    key_row = lax.broadcasted_iota(jnp.int32, (BLK, n_q), 0)
    part_max = jnp.full((1, n_q), NEG_BIG, F32)
    for k in range(NC):
        for d in range(NY):
            number = at(lax.rem(y + NY - d, NY), z, flip(k))
            visible = (key_row < lengths_s[number]) & (key_row + number * BLK <= reach)
            block_scores = dot_nt(kvb[k, d, :BLK], queries) * SCALE
            block_scores = jnp.where(visible, block_scores, NEG_BIG)
            part_max = jnp.maximum(part_max, jnp.max(block_scores, axis=0, keepdims=True))
            blocks.append((k, d, visible, block_scores))
    part_sum = jnp.zeros((1, n_q), F32)
    part_value = jnp.zeros((n_q, HEAD_DIM), F32)
    for k, d, visible, block_scores in blocks:
        block_weights = jnp.where(visible, jnp.exp(block_scores - part_max), 0.0)
        part_sum = part_sum + jnp.sum(block_weights, axis=0, keepdims=True)
        part_value = part_value + dot_tn(block_weights.astype(BF16), kvb[k, d, BLK:])
    n_r = HEADS * QROW
    stats = jnp.concatenate(
        split3(part_max) + split3(part_sum) + [jnp.zeros((10, n_q), F32)], axis=0
    ).astype(BF16)
    if n_q < LANES:
        stats = jnp.concatenate([stats, jnp.zeros((16, LANES - n_q), BF16)], axis=1)
    part[:, :n_r] = part_value.astype(BF16).reshape(NZ, n_r, HEAD_DIM)
    for d in range(NZ):
        group = d * n_r // LANES * LANES
        part[d, n_r:] = stats[:, group:group + LANES]
    part_ins = {NZ - d: send(part.at[d], part_in.at[NZ - d], z_peer(NZ - d)) for d in z_steps}

    for copy in a3_in:
        copy.wait_recv()
    a_keys = anc[:, :a_len].reshape(BLK, HEAD_DIM)
    a_values = anc[:, a_len:].reshape(BLK, HEAD_DIM)
    far = (key_at < lengths_s[anchor_block]) & (jnp.zeros_like(key_at) + anchor_block != c)
    scores = jnp.where(far, dot_nt(q4[...], a_keys) * SCALE, NEG_BIG)
    row_max = jnp.maximum(own_max, jnp.max(scores, axis=1, keepdims=True))
    weights = jnp.where(far, jnp.exp(scores - row_max), 0.0)
    own_factor = jnp.exp(own_max - row_max)
    total = jnp.sum(weights, axis=1, keepdims=True) + own_sum * own_factor
    value = dot_nn(weights.astype(BF16), a_values) + own_value * own_factor
    value = (value / total).astype(BF16)
    attended = jnp.concatenate([value[h * BLK:(h + 1) * BLK] for h in range(HEADS)], axis=1)

    def term(slot, j):
        return dot_nn(attended, w_out[slot, :, j * quarter:(j + 1) * quarter])

    wo_loads[3].wait()
    tr = {}
    for j in (0, 3, 1, 2):
        tr_out[j] = term(3, j).astype(BF16)
        tr[j] = send(tr_out.at[j], tr_in.at[j], right if j < 2 else left)
    wo_loads[2].wait()
    wo_loads[1].wait()
    final_r, final_l = {}, {}
    for j in (2, 3):
        to_right[j] = term(2, j).astype(BF16)
        final_r[j] = send(to_right.at[j], from_left.at[j], right)
        i = 3 - j
        to_left[i] = term(1, i).astype(BF16)
        final_l[i] = send(to_left.at[i], from_right.at[i], left)
    r_terms = {j: term(2, j) for j in (0, 1)}
    l_terms = {j: term(1, j) for j in (3, 2)}
    for j in (0, 1):
        tr[j].wait_recv()
        to_right[j] = (r_terms[j] + tr_in[j].astype(F32)).astype(BF16)
        final_r[j] = send(to_right.at[j], from_left.at[j], right)
        i = 3 - j
        tr[i].wait_recv()
        to_left[i] = (l_terms[i] + tr_in[i].astype(F32)).astype(BF16)
        final_l[i] = send(to_left.at[i], from_right.at[i], left)
    wo_loads[0].wait()
    own_term[...] = dot_nn(attended, w_out[0])

    eye_row = lax.broadcasted_iota(jnp.int32, (n_r, LANES), 0)
    eye_lane = lax.broadcasted_iota(jnp.int32, (n_r, LANES), 1)

    def column(rows, first, slot):
        line = rows[first:first + 1] + rows[first + 1:first + 2] + rows[first + 2:first + 3]
        spot = eye_lane == eye_row + (slot * n_r) % LANES
        return jnp.sum(jnp.where(spot, line, 0.0), axis=1, keepdims=True)

    maxima, sums, values = [], [], []
    for d in range(NZ):
        if d:
            part_ins[d].wait_recv()
        block = (part_in[d] if d else part[0]).astype(F32)
        slot = (NZ - d) % NZ
        maxima.append(column(block[n_r:], 0, slot))
        sums.append(column(block[n_r:], 3, slot))
        values.append(block[:n_r])
    top_max = maxima[0]
    for one in maxima[1:]:
        top_max = jnp.maximum(top_max, one)
    all_sum = jnp.zeros((n_r, 1), F32)
    all_value = jnp.zeros((n_r, HEAD_DIM), F32)
    for one_max, one_sum, one_value in zip(maxima, sums, values):
        factor = jnp.exp(one_max - top_max)
        all_sum = all_sum + one_sum * factor
        all_value = all_value + one_value * factor
    all_value = all_value / all_sum
    q_att = jnp.concatenate([all_value[h * QROW:(h + 1) * QROW] for h in range(HEADS)], axis=1)
    q_att = jnp.concatenate([q_att, jnp.zeros_like(q_att)], axis=0).astype(BF16)
    qx_in_copies = []
    for slot, device in ((3, opposite), (2, right), (1, left)):
        q_term = dot_nn(q_att, w_out[slot])[:QROW]
        qx_out[slot] = jnp.concatenate([q_term[:, :half_f], q_term[:, half_f:]], axis=0).astype(BF16)
        qx_in_copies.append(send(qx_out.at[slot], qx_in.at[slot], device))
    q_own = dot_nn(q_att, w_out[0])[:QROW]

    for j in (2, 1, 0, 3):
        final_r[j].wait_recv()
        final_l[j].wait_recv()
        columns = slice(j * quarter, (j + 1) * quarter)
        ctx_out[:, columns] = (
            own_term[:, columns] + from_left[j].astype(F32) + from_right[j].astype(F32)
        ).astype(BF16)
    for copy in qx_in_copies:
        copy.wait_recv()
    for slot in (1, 2, 3):
        packed = qx_in[slot].astype(F32)
        q_own = q_own + jnp.concatenate([packed[:QROW], packed[QROW:]], axis=1)
    q_out[...] = q_own.astype(BF16)
    for copy in copies:
        copy.wait_send()


def split3(x):
    high = x.astype(BF16).astype(F32)
    middle = (x - high).astype(BF16).astype(F32)
    return [high, middle, x - high - middle]


def local(tokens, questions, q_weight, k_weight, v_weight, o_weight, anchor, lengths, positions):
    n_r = HEADS * QROW
    n_p = NY * NC
    a_len = BLK // n_p
    anywhere = pl.BlockSpec(memory_space=pltpu.HBM)
    vmem = pl.BlockSpec(memory_space=pltpu.VMEM)
    smem = pl.BlockSpec(memory_space=pltpu.SMEM)
    operands = [
        pltpu.with_memory_space_constraint(x, pltpu.HBM)
        for x in (tokens, questions, q_weight, k_weight, v_weight, o_weight)
    ]
    lengths, positions = [
        pltpu.with_memory_space_constraint(x, pltpu.HBM) for x in (lengths, positions)
    ]
    return pl.pallas_call(
        kernel,
        out_shape=(
            jax.ShapeDtypeStruct((BLK, FEAT), BF16),
            jax.ShapeDtypeStruct((QROW, FEAT), BF16),
        ),
        in_specs=[anywhere] * 6 + [smem] + [anywhere] * 2,
        out_specs=(vmem, vmem),
        scratch_shapes=[
            pltpu.VMEM((QROW, FEAT), BF16),
            pltpu.SMEM(lengths.shape, jnp.int32),
            pltpu.SMEM(positions.shape, jnp.int32),
            pltpu.VMEM((NX, FEAT, WCOLS), BF16),
            pltpu.VMEM((NX, QCOLS, FEAT), BF16),
            pltpu.VMEM((BLK, FEAT), BF16),
            pltpu.VMEM((NX, 4, BLK, FEAT // 4), BF16),
            pltpu.VMEM((NX, 2 * QROW, FEAT // 2), BF16),
            pltpu.VMEM((BLK, WCOLS), F32),
            pltpu.VMEM((HEADS * BLK, HEAD_DIM), BF16),
            pltpu.VMEM((NZ, n_r, HEAD_DIM), BF16),
            pltpu.VMEM((NC, NY, 2 * BLK, HEAD_DIM), BF16),
            pltpu.VMEM((n_p, a_len, FEAT), BF16),
            pltpu.VMEM((NX, a_len, FEAT), BF16),
            pltpu.VMEM((NZ, 2 * a_len, HEAD_DIM), BF16),
            pltpu.VMEM((n_p, 2 * a_len, HEAD_DIM), BF16),
            pltpu.VMEM((NZ, n_r + 16, HEAD_DIM), BF16),
            pltpu.VMEM((NZ, n_r + 16, HEAD_DIM), BF16),
            pltpu.VMEM((4, BLK, FEAT // 4), BF16),
            pltpu.VMEM((4, BLK, FEAT // 4), BF16),
            pltpu.VMEM((4, BLK, FEAT // 4), BF16),
            pltpu.VMEM((4, BLK, FEAT // 4), BF16),
            pltpu.VMEM((4, BLK, FEAT // 4), BF16),
            pltpu.VMEM((4, BLK, FEAT // 4), BF16),
            pltpu.VMEM((BLK, FEAT), F32),
            pltpu.VMEM((NX, 2 * QROW, FEAT // 2), BF16),
            pltpu.VMEM((NX, 2 * QROW, FEAT // 2), BF16),
            pltpu.SemaphoreType.DMA((N_LOADS,)),
            pltpu.SemaphoreType.DMA((N_COPIES,)),
            pltpu.SemaphoreType.DMA((N_COPIES,)),
        ],
        compiler_params=pltpu.CompilerParams(
            collective_id=0, has_side_effects=True, vmem_limit_bytes=40 * 2**20
        ),
        name="fused_attention",
    )(*operands, anchor, lengths, positions)


def solution(mesh):
    in_specs = (
        P("ctx", "kvg"),
        P("ctx", "kvg"),
        P(None, "kvg"),
        P(None, "kvg"),
        P(None, "kvg"),
        P("kvg", None),
        P(),
        P(),
        P(),
    )
    out_specs = (P("ctx", "kvg"), P("ctx", "kvg"))
    return jax.shard_map(local, mesh=mesh, in_specs=in_specs, out_specs=out_specs, check_vma=False)
```

time: 50.6 us -> 47.6 us (0.941)
  Pallas kernels: 47.8 us -> 44.8 us
    pallas_call x1, Pallas kernels: 47.8 us -> 44.8 us  [local(): pl.pallas_call(kernel, out_shape=(jax.ShapeDtypeStruct((BLK, FEAT), BF16)...]
where the time goes in v3:
time: 47.6 us; the launch traced here: 47.4 us
  Pallas kernels  44.8 us (94%)
  local copies, waits for them, and re-layouts  1.31 us (3%)
  between operations  1.29 us (3%)
    pallas_call x1, Pallas kernels, local(): pl.pallas_call(kernel, out_shape=(jax.ShapeDtypeStruct((BLK, FEAT), BF16)...  44.8 us
    unnamed x2, local copies, waits for them, and re-layouts  1.31 us

profile of v3, /device:TPU:1, one launch (start us, length us, event | category | flops | bytes accessed | tf_op | source)
XLA Modules:
  0.0 47.4 jit_solution(12174194262576908235)
XLA Ops:
  1.3 44.8 %fused_attention.1 = (bf16[128,1024]{1,0:T(8,128)(2,1)S(1)}, bf16[8,1024]{1,0:T(8,128)(2,1)S(1)}) custom-call(bf16[128,1024]{1,0:T(8,128)(2,1)} %tokens.1, bf16[8,1024]{1,0:T(8,128)(2,1)} %questions.1, bf16[4096,512]{1,0:T(8,128)(2,1)} %wq.1, bf16[4096,128]{1,0:T(8,128)(2,1)} %wk.1, bf16[4096,128]{1,0:T(8,128)(2,1)} %wv.1, bf16[512,4096]{1,0:T(8,128)(2,1)} %wo.1, ...), custom_call_target="tpu_custom_call" | custom-call | tf_op jit(solution)/shard_map/fused_attention/pallas_call | solution.py:447
  46.1 0.7 %copy.14 = bf16[128,1024]{1,0:T(8,128)(2,1)} copy(bf16[128,1024]{1,0:T(8,128)(2,1)S(1)} %get-tuple-element.4) | data formatting | bytes 524288
  46.8 0.6 %copy.15 = bf16[8,1024]{1,0:T(8,128)(2,1)} copy(bf16[8,1024]{1,0:T(8,128)(2,1)S(1)} %get-tuple-element.5) | data formatting | bytes 32768

commit v4 on v3

--- a/solution.py
+++ b/solution.py
@@ -90,6 +90,12 @@
     def z_peer(d):
         return (at(y, lax.rem(z + d, NZ), core), g)
 
+    partners = [z_peer(d) for d in z_steps] + [opposite]
+    partners += [p_peer(dy, dc) for dy, dc in p_steps] + [left, right]
+    barrier = pltpu.get_barrier_semaphore()
+    for partner in partners:
+        pl.semaphore_signal(barrier, inc=1, device_id=partner, device_id_type=MESH)
+
     loads = []
 
     def load(source, target):
@@ -110,12 +116,6 @@
             load(wv.at[rows, :], w_in.at[slot, :, pl.ds(QCOLS + HEAD_DIM, HEAD_DIM)]),
         ])
 
-    partners = [z_peer(d) for d in z_steps] + [opposite]
-    partners += [p_peer(dy, dc) for dy, dc in p_steps] + [left, right]
-    barrier = pltpu.get_barrier_semaphore()
-    for partner in partners:
-        pl.semaphore_signal(barrier, inc=1, device_id=partner, device_id_type=MESH)
-
     asked_load.wait()
     own_questions = asked[...].astype(F32)
     half_f = FEAT // 2
@@ -149,13 +149,6 @@
         there = pl.ds(pl.multiple_of(p_index(dy, dc) * a_len, a_len), a_len)
         a_in[dy, dc] = send(tokens.at[there, :], a_rows.at[dy * NC + dc], p_peer(dy, dc))
     send_tokens(1, 2)
-    send_tokens(2, 1)
-    send_tokens(3, 0)
-    q_in = [
-        send(qpack.at[0], qpack.at[3], opposite),
-        send(qpack.at[0], qpack.at[1], right),
-        send(qpack.at[0], qpack.at[2], left),
-    ]
 
     tok_load.wait()
     for copy in w_loads[0]:
@@ -163,6 +156,7 @@
     acc[...] = dot_nn(own_tok[...], w_in[0])
     row = lax.broadcasted_iota(jnp.int32, (BLK, HEAD_DIM), 0)
     cosine, sine = angles(row + c * BLK)
+    send_tokens(2, 1)
     for copy in scalar_loads:
         copy.wait()
     q_row = lax.broadcasted_iota(jnp.int32, (QROW, HEAD_DIM), 0)
@@ -176,17 +170,16 @@
     anchor_z = lax.rem(lax.div(anchor_block, NC), NZ)
     a_row = lax.broadcasted_iota(jnp.int32, (a_len, HEAD_DIM), 0)
     a_cosine, a_sine = angles(a_row + p * a_len + anchor_block * BLK)
-
-    far_r, far_l = {}, {}
-
-    def pass_on(j_r, j_l):
-        near_r[j_r].wait_recv()
-        far_r[j_r] = send(tok.at[1, j_r], tok.at[3, j_r], right)
-        near_l[j_l].wait_recv()
-        far_l[j_l] = send(tok.at[2, j_l], tok.at[3, j_l], left)
-
-    pass_on(0, 3)
-    pass_on(1, 2)
+    send_tokens(3, 0)
+
+    n_q = NZ * HEADS * QROW
+    lane = lax.broadcasted_iota(jnp.int32, (1, n_q), 1)
+    reach = jnp.zeros((1, n_q), jnp.int32)
+    for d in range(NZ):
+        there = at(y, lax.rem(z + NZ - d, NZ), core) * QROW
+        for r in range(QROW):
+            spot = (lax.div(lane, HEADS * QROW) == d) & (lax.rem(lane, QROW) == r)
+            reach = jnp.where(spot, positions_s[there + r], reach)
 
     wanted = jnp.zeros((a_len, FEAT), jnp.int32)
     wanted_p = wanted + (anchor_y * NC + anchor_core)
@@ -202,6 +195,22 @@
         send(a_tok.at[0], a_tok.at[2], left),
     ]
 
+    far_r, far_l = {}, {}
+
+    def pass_on(j_r, j_l):
+        near_r[j_r].wait_recv()
+        far_r[j_r] = send(tok.at[1, j_r], tok.at[3, j_r], right)
+        near_l[j_l].wait_recv()
+        far_l[j_l] = send(tok.at[2, j_l], tok.at[3, j_l], left)
+
+    pass_on(0, 3)
+    pass_on(1, 2)
+    q_in = [
+        send(qpack.at[0], qpack.at[3], opposite),
+        send(qpack.at[0], qpack.at[1], right),
+        send(qpack.at[0], qpack.at[2], left),
+    ]
+
     for slot in (1, 2):
         for copy in w_loads[slot]:
             copy.wait()
@@ -209,6 +218,21 @@
         acc[...] += dot_nn(tok[1, j], w_in[1, j * quarter:(j + 1) * quarter])
         k = 3 - j
         acc[...] += dot_nn(tok[2, k], w_in[2, k * quarter:(k + 1) * quarter])
+    for copy in w_loads[3]:
+        copy.wait()
+    for copy in at_in:
+        copy.wait_recv()
+    a_kv = jnp.zeros((a_len, 2 * HEAD_DIM), F32)
+    for slot in range(NX):
+        a_kv = a_kv + dot_nn(a_tok[slot], w_in[slot, :, QCOLS:])
+    a2[0, :a_len] = rotate(a_kv[:, :HEAD_DIM], a_cosine, a_sine).astype(BF16)
+    a2[0, a_len:] = a_kv[:, HEAD_DIM:].astype(BF16)
+    a2_in = {d: send(a2.at[0], a2.at[d], z_peer(d)) for d in z_steps}
+    wo_loads = {}
+    for slot in (3, 2, 1, 0):
+        columns = pl.ds(pl.multiple_of(src[slot] * FEAT, FEAT), FEAT)
+        wo_loads[slot] = load(wo.at[:, columns], w_out.at[slot])
+
     for j in range(2, 4):
         near_r[j].wait_recv()
         acc[...] += dot_nn(tok[1, j], w_in[1, j * quarter:(j + 1) * quarter])
@@ -216,8 +240,19 @@
         near_l[k].wait_recv()
         acc[...] += dot_nn(tok[2, k], w_in[2, k * quarter:(k + 1) * quarter])
 
-    for copy in w_loads[3]:
-        copy.wait()
+    for j in (0, 3, 1):
+        (far_r if j < 2 else far_l)[j].wait_recv()
+        acc[...] += dot_nn(tok[3, j], w_in[3, j * quarter:(j + 1) * quarter])
+    far_l[2].wait_recv()
+    last_rows = slice(2 * quarter, 3 * quarter)
+    key_value = acc[:, QCOLS:] + dot_nn(tok[3, 2], w_in[3, last_rows, QCOLS:])
+    kvb[0, 0, :BLK] = rotate(key_value[:, :HEAD_DIM], cosine, sine).astype(BF16)
+    kvb[0, 0, BLK:] = key_value[:, HEAD_DIM:].astype(BF16)
+    kv_in = [
+        send(kvb.at[0, 0], kvb.at[0, d], p_peer(d, 0))
+        for d in sorted(range(1, NY), key=lambda d: -min(d, NY - d))
+    ]
+
     for copy in q_in:
         copy.wait_recv()
     q_total = jnp.zeros((2 * QROW, QCOLS), F32)
@@ -233,36 +268,19 @@
     qz[0] = jnp.concatenate(q_heads, axis=0).astype(BF16)
     qz_in = [send(qz.at[0], qz.at[d], z_peer(d)) for d in z_steps]
 
-    key_value = acc[:, QCOLS:]
-    for j in (0, 3, 1, 2):
-        (far_r if j < 2 else far_l)[j].wait_recv()
-        key_value = key_value + dot_nn(tok[3, j], w_in[3, j * quarter:(j + 1) * quarter, QCOLS:])
-    kvb[0, 0, :BLK] = rotate(key_value[:, :HEAD_DIM], cosine, sine).astype(BF16)
-    kvb[0, 0, BLK:] = key_value[:, HEAD_DIM:].astype(BF16)
-
-    for copy in at_in:
-        copy.wait_recv()
-    a_kv = jnp.zeros((a_len, 2 * HEAD_DIM), F32)
-    for slot in range(NX):
-        a_kv = a_kv + dot_nn(a_tok[slot], w_in[slot, :, QCOLS:])
-    a2[0, :a_len] = rotate(a_kv[:, :HEAD_DIM], a_cosine, a_sine).astype(BF16)
-    a2[0, a_len:] = a_kv[:, HEAD_DIM:].astype(BF16)
-    a2_in = {d: send(a2.at[0], a2.at[d], z_peer(d)) for d in z_steps}
-    kv_in = [
-        send(kvb.at[0, 0], kvb.at[0, d], p_peer(d, 0))
-        for d in sorted(range(1, NY), key=lambda d: -min(d, NY - d))
-    ]
-    wo_loads = {}
-    for slot in (3, 2, 1, 0):
-        columns = pl.ds(pl.multiple_of(src[slot] * FEAT, FEAT), FEAT)
-        wo_loads[slot] = load(wo.at[:, columns], w_out.at[slot])
-
+    wanted_z = jnp.zeros((2 * a_len, HEAD_DIM), jnp.int32) + anchor_z
+    chosen = a2[0].astype(F32)
+    for d in z_steps:
+        a2_in[d].wait_recv()
+        origin = lax.rem(z + NZ - d, NZ)
+        chosen = jnp.where(wanted_z == origin, a2[d].astype(F32), chosen)
+    anc[p] = chosen.astype(BF16)
+    a3_in = [send(anc.at[p], anc.at[p], p_peer(dy, dc)) for dy, dc in p_steps]
+
+    query = acc[:, :QCOLS] + dot_nn(tok[3, 2], w_in[3, last_rows, :QCOLS])
     for h in range(HEADS):
-        columns = slice(h * HEAD_DIM, (h + 1) * HEAD_DIM)
-        query = acc[:, columns]
-        for j in range(4):
-            query = query + dot_nn(tok[3, j], w_in[3, j * quarter:(j + 1) * quarter, columns])
-        q4[h * BLK:(h + 1) * BLK] = rotate(query, cosine, sine).astype(BF16)
+        head = query[:, h * HEAD_DIM:(h + 1) * HEAD_DIM]
+        q4[h * BLK:(h + 1) * BLK] = rotate(head, cosine, sine).astype(BF16)
     key_at = lax.broadcasted_iota(jnp.int32, (HEADS * BLK, BLK), 1)
     query_at = lax.rem(lax.broadcasted_iota(jnp.int32, (HEADS * BLK, BLK), 0), BLK)
     seen = (key_at <= query_at) & (key_at < lengths_s[c])
@@ -272,26 +290,47 @@
     own_sum = jnp.sum(weights, axis=1, keepdims=True)
     own_value = dot_nn(weights.astype(BF16), kvb[0, 0, BLK:])
 
-    n_q = NZ * HEADS * QROW
-    lane = lax.broadcasted_iota(jnp.int32, (1, n_q), 1)
-    reach = jnp.zeros((1, n_q), jnp.int32)
-    for d in range(NZ):
-        there = at(y, lax.rem(z + NZ - d, NZ), core) * QROW
-        for r in range(QROW):
-            spot = (lax.div(lane, HEADS * QROW) == d) & (lax.rem(lane, QROW) == r)
-            reach = jnp.where(spot, positions_s[there + r], reach)
-
+    done = len(copies)
+    for copy in copies[:done - len(a3_in)]:
+        copy.wait_send()
+    done -= len(a3_in)
+
+    for copy in a3_in:
+        copy.wait_recv()
+    a_keys = anc[:, :a_len].reshape(BLK, HEAD_DIM)
+    a_values = anc[:, a_len:].reshape(BLK, HEAD_DIM)
+    far = (key_at < lengths_s[anchor_block]) & (jnp.zeros_like(key_at) + anchor_block != c)
+    scores = jnp.where(far, dot_nt(q4[...], a_keys) * SCALE, NEG_BIG)
+    row_max = jnp.maximum(own_max, jnp.max(scores, axis=1, keepdims=True))
+    weights = jnp.where(far, jnp.exp(scores - row_max), 0.0)
+    own_factor = jnp.exp(own_max - row_max)
+    total = jnp.sum(weights, axis=1, keepdims=True) + own_sum * own_factor
+    value = dot_nn(weights.astype(BF16), a_values) + own_value * own_factor
+    value = (value / total).astype(BF16)
+    attended = jnp.concatenate([value[h * BLK:(h + 1) * BLK] for h in range(HEADS)], axis=1)
+
+    def term(slot, j):
+        return dot_nn(attended, w_out[slot, :, j * quarter:(j + 1) * quarter])
+
+    wo_loads[3].wait()
+    tr = {}
+    for j in (0, 3, 1, 2):
+        tr_out[j] = term(3, j).astype(BF16)
+        tr[j] = send(tr_out.at[j], tr_in.at[j], right if j < 2 else left)
     for copy in kv_in:
         copy.wait_recv()
     sib_in = send(kvb.at[0], kvb.at[1], (at(y, z, 1 - core), g)) if NC > 1 else None
-    wanted_z = jnp.zeros((2 * a_len, HEAD_DIM), jnp.int32) + anchor_z
-    chosen = a2[0].astype(F32)
-    for d in z_steps:
-        a2_in[d].wait_recv()
-        origin = lax.rem(z + NZ - d, NZ)
-        chosen = jnp.where(wanted_z == origin, a2[d].astype(F32), chosen)
-    anc[p] = chosen.astype(BF16)
-    a3_in = [send(anc.at[p], anc.at[p], p_peer(dy, dc)) for dy, dc in p_steps]
+    wo_loads[2].wait()
+    wo_loads[1].wait()
+    final_r, final_l = {}, {}
+    for j in (2, 3):
+        to_right[j] = term(2, j).astype(BF16)
+        final_r[j] = send(to_right.at[j], from_left.at[j], right)
+        i = 3 - j
+        to_left[i] = term(1, i).astype(BF16)
+        final_l[i] = send(to_left.at[i], from_right.at[i], left)
+    r_terms = {j: term(2, j) for j in (0, 1)}
+    l_terms = {j: term(1, j) for j in (3, 2)}
 
     for copy in qz_in:
         copy.wait_recv()
@@ -327,39 +366,6 @@
         part[d, n_r:] = stats[:, group:group + LANES]
     part_ins = {NZ - d: send(part.at[d], part_in.at[NZ - d], z_peer(NZ - d)) for d in z_steps}
 
-    for copy in a3_in:
-        copy.wait_recv()
-    a_keys = anc[:, :a_len].reshape(BLK, HEAD_DIM)
-    a_values = anc[:, a_len:].reshape(BLK, HEAD_DIM)
-    far = (key_at < lengths_s[anchor_block]) & (jnp.zeros_like(key_at) + anchor_block != c)
-    scores = jnp.where(far, dot_nt(q4[...], a_keys) * SCALE, NEG_BIG)
-    row_max = jnp.maximum(own_max, jnp.max(scores, axis=1, keepdims=True))
-    weights = jnp.where(far, jnp.exp(scores - row_max), 0.0)
-    own_factor = jnp.exp(own_max - row_max)
-    total = jnp.sum(weights, axis=1, keepdims=True) + own_sum * own_factor
-    value = dot_nn(weights.astype(BF16), a_values) + own_value * own_factor
-    value = (value / total).astype(BF16)
-    attended = jnp.concatenate([value[h * BLK:(h + 1) * BLK] for h in range(HEADS)], axis=1)
-
-    def term(slot, j):
-        return dot_nn(attended, w_out[slot, :, j * quarter:(j + 1) * quarter])
-
-    wo_loads[3].wait()
-    tr = {}
-    for j in (0, 3, 1, 2):
-        tr_out[j] = term(3, j).astype(BF16)
-        tr[j] = send(tr_out.at[j], tr_in.at[j], right if j < 2 else left)
-    wo_loads[2].wait()
-    wo_loads[1].wait()
-    final_r, final_l = {}, {}
-    for j in (2, 3):
-        to_right[j] = term(2, j).astype(BF16)
-        final_r[j] = send(to_right.at[j], from_left.at[j], right)
-        i = 3 - j
-        to_left[i] = term(1, i).astype(BF16)
-        final_l[i] = send(to_left.at[i], from_right.at[i], left)
-    r_terms = {j: term(2, j) for j in (0, 1)}
-    l_terms = {j: term(1, j) for j in (3, 2)}
     for j in (0, 1):
         tr[j].wait_recv()
         to_right[j] = (r_terms[j] + tr_in[j].astype(F32)).astype(BF16)
@@ -420,7 +426,7 @@
         packed = qx_in[slot].astype(F32)
         q_own = q_own + jnp.concatenate([packed[:QROW], packed[QROW:]], axis=1)
     q_out[...] = q_own.astype(BF16)
-    for copy in copies:
+    for copy in copies[done:]:
         copy.wait_send()
 
 

time: 47.6 us -> 46.1 us (0.968)
  Pallas kernels: 44.8 us -> 43.4 us
    pallas_call x1, Pallas kernels: 44.8 us -> 43.4 us  [local(): pl.pallas_call(kernel, out_shape=(jax.ShapeDtypeStruct((BLK, FEAT), BF16)...]
where the time goes in v4:
time: 46.1 us; the launch traced here: 46 us
  Pallas kernels  43.4 us (94%)
  local copies, waits for them, and re-layouts  1.31 us (3%)
  between operations  1.29 us (3%)
    pallas_call x1, Pallas kernels, local(): pl.pallas_call(kernel, out_shape=(jax.ShapeDtypeStruct((BLK, FEAT), BF16)...  43.4 us
    unnamed x2, local copies, waits for them, and re-layouts  1.31 us

profile of v4, /device:TPU:1, one launch (start us, length us, event | category | flops | bytes accessed | tf_op | source)
XLA Modules:
  0.0 46.0 jit_solution(161725733876385412)
XLA Ops:
  1.3 43.4 %fused_attention.1 = (bf16[128,1024]{1,0:T(8,128)(2,1)S(1)}, bf16[8,1024]{1,0:T(8,128)(2,1)S(1)}) custom-call(bf16[128,1024]{1,0:T(8,128)(2,1)} %tokens.1, bf16[8,1024]{1,0:T(8,128)(2,1)} %questions.1, bf16[4096,512]{1,0:T(8,128)(2,1)} %wq.1, bf16[4096,128]{1,0:T(8,128)(2,1)} %wk.1, bf16[4096,128]{1,0:T(8,128)(2,1)} %wv.1, bf16[512,4096]{1,0:T(8,128)(2,1)} %wo.1, ...), custom_call_target="tpu_custom_call" | custom-call | tf_op jit(solution)/shard_map/fused_attention/pallas_call | solution.py:453
  44.7 0.7 %copy.14 = bf16[128,1024]{1,0:T(8,128)(2,1)} copy(bf16[128,1024]{1,0:T(8,128)(2,1)S(1)} %get-tuple-element.4) | data formatting | bytes 524288
  45.4 0.6 %copy.15 = bf16[8,1024]{1,0:T(8,128)(2,1)} copy(bf16[8,1024]{1,0:T(8,128)(2,1)S(1)} %get-tuple-element.5) | data formatting | bytes 32768

commit v5 on v4

--- a/solution.py
+++ b/solution.py
@@ -170,7 +170,6 @@
     anchor_z = lax.rem(lax.div(anchor_block, NC), NZ)
     a_row = lax.broadcasted_iota(jnp.int32, (a_len, HEAD_DIM), 0)
     a_cosine, a_sine = angles(a_row + p * a_len + anchor_block * BLK)
-    send_tokens(3, 0)
 
     n_q = NZ * HEADS * QROW
     lane = lax.broadcasted_iota(jnp.int32, (1, n_q), 1)
@@ -194,6 +193,8 @@
         send(a_tok.at[0], a_tok.at[1], right),
         send(a_tok.at[0], a_tok.at[2], left),
     ]
+
+    send_tokens(3, 0)
 
     far_r, far_l = {}, {}
 
@@ -290,10 +291,13 @@
     own_sum = jnp.sum(weights, axis=1, keepdims=True)
     own_value = dot_nn(weights.astype(BF16), kvb[0, 0, BLK:])
 
-    done = len(copies)
-    for copy in copies[:done - len(a3_in)]:
+    for copy in kv_in:
+        copy.wait_recv()
+    sib_in = send(kvb.at[0], kvb.at[1], (at(y, z, 1 - core), g)) if NC > 1 else None
+
+    done = len(copies) - len(a3_in) - 1
+    for copy in copies[:done]:
         copy.wait_send()
-    done -= len(a3_in)
 
     for copy in a3_in:
         copy.wait_recv()
@@ -317,21 +321,6 @@
     for j in (0, 3, 1, 2):
         tr_out[j] = term(3, j).astype(BF16)
         tr[j] = send(tr_out.at[j], tr_in.at[j], right if j < 2 else left)
-    for copy in kv_in:
-        copy.wait_recv()
-    sib_in = send(kvb.at[0], kvb.at[1], (at(y, z, 1 - core), g)) if NC > 1 else None
-    wo_loads[2].wait()
-    wo_loads[1].wait()
-    final_r, final_l = {}, {}
-    for j in (2, 3):
-        to_right[j] = term(2, j).astype(BF16)
-        final_r[j] = send(to_right.at[j], from_left.at[j], right)
-        i = 3 - j
-        to_left[i] = term(1, i).astype(BF16)
-        final_l[i] = send(to_left.at[i], from_right.at[i], left)
-    r_terms = {j: term(2, j) for j in (0, 1)}
-    l_terms = {j: term(1, j) for j in (3, 2)}
-
     for copy in qz_in:
         copy.wait_recv()
     queries = qz[...].reshape(n_q, HEAD_DIM)
@@ -366,6 +355,18 @@
         part[d, n_r:] = stats[:, group:group + LANES]
     part_ins = {NZ - d: send(part.at[d], part_in.at[NZ - d], z_peer(NZ - d)) for d in z_steps}
 
+    wo_loads[2].wait()
+    wo_loads[1].wait()
+    final_r, final_l = {}, {}
+    for j in (2, 3):
+        to_right[j] = term(2, j).astype(BF16)
+        final_r[j] = send(to_right.at[j], from_left.at[j], right)
+        i = 3 - j
+        to_left[i] = term(1, i).astype(BF16)
+        final_l[i] = send(to_left.at[i], from_right.at[i], left)
+    r_terms = {j: term(2, j) for j in (0, 1)}
+    l_terms = {j: term(1, j) for j in (3, 2)}
+
     for j in (0, 1):
         tr[j].wait_recv()
         to_right[j] = (r_terms[j] + tr_in[j].astype(F32)).astype(BF16)
@@ -374,9 +375,6 @@
         tr[i].wait_recv()
         to_left[i] = (l_terms[i] + tr_in[i].astype(F32)).astype(BF16)
         final_l[i] = send(to_left.at[i], from_right.at[i], left)
-    wo_loads[0].wait()
-    own_term[...] = dot_nn(attended, w_out[0])
-
     eye_row = lax.broadcasted_iota(jnp.int32, (n_r, LANES), 0)
     eye_lane = lax.broadcasted_iota(jnp.int32, (n_r, LANES), 1)
 
@@ -411,7 +409,10 @@
         q_term = dot_nn(q_att, w_out[slot])[:QROW]
         qx_out[slot] = jnp.concatenate([q_term[:, :half_f], q_term[:, half_f:]], axis=0).astype(BF16)
         qx_in_copies.append(send(qx_out.at[slot], qx_in.at[slot], device))
+    wo_loads[0].wait()
     q_own = dot_nn(q_att, w_out[0])[:QROW]
+
+    own_term[...] = dot_nn(attended, w_out[0])
 
     for j in (2, 1, 0, 3):
         final_r[j].wait_recv()

time: 46.1 us -> 44.7 us (0.970)
  Pallas kernels: 43.4 us -> 42 us
    pallas_call x1, Pallas kernels: 43.4 us -> 42 us  [local(): pl.pallas_call(kernel, out_shape=(jax.ShapeDtypeStruct((BLK, FEAT), BF16)...]
where the time goes in v5:
time: 44.7 us; the launch traced here: 44.6 us
  Pallas kernels  42 us (94%)
  local copies, waits for them, and re-layouts  1.31 us (3%)
  between operations  1.29 us (3%)
    pallas_call x1, Pallas kernels, local(): pl.pallas_call(kernel, out_shape=(jax.ShapeDtypeStruct((BLK, FEAT), BF16)...  42 us
    unnamed x2, local copies, waits for them, and re-layouts  1.31 us

profile of v5, /device:TPU:1, one launch (start us, length us, event | category | flops | bytes accessed | tf_op | source)
XLA Modules:
  0.0 44.6 jit_solution(728879014392121456)
XLA Ops:
  1.3 42.0 %fused_attention.1 = (bf16[128,1024]{1,0:T(8,128)(2,1)S(1)}, bf16[8,1024]{1,0:T(8,128)(2,1)S(1)}) custom-call(bf16[128,1024]{1,0:T(8,128)(2,1)} %tokens.1, bf16[8,1024]{1,0:T(8,128)(2,1)} %questions.1, bf16[4096,512]{1,0:T(8,128)(2,1)} %wq.1, bf16[4096,128]{1,0:T(8,128)(2,1)} %wk.1, bf16[4096,128]{1,0:T(8,128)(2,1)} %wv.1, bf16[512,4096]{1,0:T(8,128)(2,1)} %wo.1, ...), custom_call_target="tpu_custom_call" | custom-call | tf_op jit(solution)/shard_map/fused_attention/pallas_call | solution.py:454
  43.3 0.7 %copy.14 = bf16[128,1024]{1,0:T(8,128)(2,1)} copy(bf16[128,1024]{1,0:T(8,128)(2,1)S(1)} %get-tuple-element.4) | data formatting | bytes 524288
  44.0 0.6 %copy.15 = bf16[8,1024]{1,0:T(8,128)(2,1)} copy(bf16[8,1024]{1,0:T(8,128)(2,1)S(1)} %get-tuple-element.5) | data formatting | bytes 32768

commit v6 on v5

--- a/solution.py
+++ b/solution.py
@@ -253,6 +253,8 @@
         send(kvb.at[0, 0], kvb.at[0, d], p_peer(d, 0))
         for d in sorted(range(1, NY), key=lambda d: -min(d, NY - d))
     ]
+    sibling = (at(y, z, 1 - core), g)
+    sib_own = send(kvb.at[0, 0], kvb.at[1, 0], sibling)
 
     for copy in q_in:
         copy.wait_recv()
@@ -291,9 +293,12 @@
     own_sum = jnp.sum(weights, axis=1, keepdims=True)
     own_value = dot_nn(weights.astype(BF16), kvb[0, 0, BLK:])
 
+    for copy in qz_in:
+        copy.wait_recv()
     for copy in kv_in:
         copy.wait_recv()
-    sib_in = send(kvb.at[0], kvb.at[1], (at(y, z, 1 - core), g)) if NC > 1 else None
+    rest = pl.ds(1, NY - 1)
+    sib_in = send(kvb.at[0, rest], kvb.at[1, rest], sibling)
 
     done = len(copies) - len(a3_in) - 1
     for copy in copies[:done]:
@@ -321,11 +326,9 @@
     for j in (0, 3, 1, 2):
         tr_out[j] = term(3, j).astype(BF16)
         tr[j] = send(tr_out.at[j], tr_in.at[j], right if j < 2 else left)
-    for copy in qz_in:
-        copy.wait_recv()
     queries = qz[...].reshape(n_q, HEAD_DIM)
-    if sib_in is not None:
-        sib_in.wait_recv()
+    sib_own.wait_recv()
+    sib_in.wait_recv()
     blocks = []
     key_row = lax.broadcasted_iota(jnp.int32, (BLK, n_q), 0)
     part_max = jnp.full((1, n_q), NEG_BIG, F32)

time: 44.7 us -> 45 us (level)
  no operation moved by 1% of the time
where the time goes in v6:
time: 45 us; the launch traced here: 44.8 us
  Pallas kernels  42.2 us (94%)
  local copies, waits for them, and re-layouts  1.31 us (3%)
  between operations  1.29 us (3%)
    pallas_call x1, Pallas kernels, local(): pl.pallas_call(kernel, out_shape=(jax.ShapeDtypeStruct((BLK, FEAT), BF16)...  42.2 us
    unnamed x2, local copies, waits for them, and re-layouts  1.31 us

profile of v6, /device:TPU:1, one launch (start us, length us, event | category | flops | bytes accessed | tf_op | source)
XLA Modules:
  0.0 44.8 jit_solution(2575843311543971069)
XLA Ops:
  1.3 42.2 %fused_attention.1 = (bf16[128,1024]{1,0:T(8,128)(2,1)S(1)}, bf16[8,1024]{1,0:T(8,128)(2,1)S(1)}) custom-call(bf16[128,1024]{1,0:T(8,128)(2,1)} %tokens.1, bf16[8,1024]{1,0:T(8,128)(2,1)} %questions.1, bf16[4096,512]{1,0:T(8,128)(2,1)} %wq.1, bf16[4096,128]{1,0:T(8,128)(2,1)} %wk.1, bf16[4096,128]{1,0:T(8,128)(2,1)} %wv.1, bf16[512,4096]{1,0:T(8,128)(2,1)} %wo.1, ...), custom_call_target="tpu_custom_call" | custom-call | tf_op jit(solution)/shard_map/fused_attention/pallas_call | solution.py:457
  43.5 0.7 %copy.14 = bf16[128,1024]{1,0:T(8,128)(2,1)} copy(bf16[128,1024]{1,0:T(8,128)(2,1)S(1)} %get-tuple-element.4) | data formatting | bytes 524288
  44.2 0.6 %copy.15 = bf16[8,1024]{1,0:T(8,128)(2,1)} copy(bf16[8,1024]{1,0:T(8,128)(2,1)S(1)} %get-tuple-element.5) | data formatting | bytes 32768
